TPU v7x, 32 devices: a whole 2x2x4 slice. The times are simulated.
32 devices in a mesh: dp: 8 (over y, x, core), chan: 4 (over z).
Axes of the slice: x: 2, y: 2, z: 4, core: 2. Of those that a mesh axis runs over, the one named last changes fastest.
Arguments:
- images: bfloat16 [128, 128, 1024], P('chan', 'dp'), may hold values from -6 to 6
- student_master: float32 [1152, 256], P('dp', 'chan'), may hold values from -1 to 1
- regress_master: float32 [1152, 192], P('dp', 'chan'), may hold values from -1 to 1
- teacher_weight: bfloat16 [1152, 384], P(None, 'chan'), may hold values from -0.1875 to 0.1875
- student_win: int32 [128, 128, 1024], P('chan', 'dp'), may hold values from 0 to 1
- teacher_win: int32 [192, 128, 1024], P('chan', 'dp'), may hold values from 0 to 1
- pool_win: int32 [128, 128, 256], P('chan', 'dp'), may hold values from 0 to 3
- hint_mask: int32 [128, 1024], P('dp'), may hold values from 0 to 1, as said below
- cotangent: bfloat16 [128, 128, 256], P('chan', 'dp'), may hold values from -6 to 6
- mom_student: float32 [1152, 256], P('dp', 'chan'), may hold values from -96 to 96
- sq_student: float32 [1152, 256], P('dp', 'chan'), as said below
- ema_student: float32 [1152, 256], P('dp', 'chan'), may hold values from -0.1875 to 0.1875
- mom_regress: float32 [1152, 192], P('dp', 'chan'), may hold values from -96 to 96
- sq_regress: float32 [1152, 192], P('dp', 'chan'), as said below
- ema_regress: float32 [1152, 192], P('dp', 'chan'), may hold values from -0.1875 to 0.1875
Outputs:
- pooled: bfloat16 [128, 128, 256], P('chan', 'dp')
- image_grad: bfloat16 [128, 128, 1024], P('chan', 'dp')
- new_student: float32 [1152, 256], P('dp', 'chan')
- new_mom_student: float32 [1152, 256], P('dp', 'chan')
- new_sq_student: float32 [1152, 256], P('dp', 'chan')
- new_ema_student: float32 [1152, 256], P('dp', 'chan')
- low_student: bfloat16 [1152, 256], P('dp', 'chan')
- new_regress: float32 [1152, 192], P('dp', 'chan')
- new_mom_regress: float32 [1152, 192], P('dp', 'chan')
- new_sq_regress: float32 [1152, 192], P('dp', 'chan')
- new_ema_regress: float32 [1152, 192], P('dp', 'chan')
- low_regress: bfloat16 [1152, 192], P('dp', 'chan')
- trust_norms: float32 [2, 2], replicated
Inputs may be any that keep to these rules, and one draw needn't show every extreme that they name: `hint_mask`: pixels whose index is a multiple of 4 are always 1. `sq_student`: Positive. `sq_regress`: Positive.
All inputs are finite; a program needn't handle non-finite values.
Results may differ from a plain program's by a relative error of at most 0.0067.
Values may be sent and summed in bfloat16 or wider, within the bound.
A program may use at most 128 MiB of HBM per device.

v0:
```python
import jax
import jax.numpy as jnp
from jax import lax
from jax.sharding import PartitionSpec as P

IMG = 32
STEP = 10


HINT_WEIGHT = 0.1
LEARN_RATE = 0.5
BETA_ONE = 0.9
BETA_TWO = 0.999
EPSILON = 1e-06
DECAY = 0.01
EMA_KEEP = 0.75


def convolve(inputs, weights):
    channels, batch_len, pixels = inputs.shape
    left_view = inputs.reshape(channels, batch_len, IMG, IMG)
    kernel = weights.reshape(3, 3, channels, weights.shape[1])
    result = lax.conv_general_dilated(
        left_view,
        kernel,
        (1, 1),
        ((1, 1), (1, 1)),
        dimension_numbers=("CNHW", "HWIO", "CNHW"),
        preferred_element_type=jnp.float32,
    )
    return result.reshape(result.shape[0], batch_len, pixels)


def filter_grad(inputs, grads):
    channels, batch_len, pixels = inputs.shape
    outputs_len = grads.shape[0]
    left_view = inputs.reshape(channels, batch_len, IMG, IMG)
    grad_view = grads.reshape(outputs_len, batch_len, IMG, IMG)
    result = lax.conv_general_dilated(
        left_view,
        grad_view,
        (1, 1),
        ((1, 1), (1, 1)),
        dimension_numbers=("NCHW", "OIHW", "NCHW"),
        preferred_element_type=jnp.float32,
    )
    return result.transpose(2, 3, 0, 1).reshape(9 * channels, outputs_len)


def input_grad(grads, weights):
    outputs_len, batch_len, pixels = grads.shape
    channels = weights.shape[0] // 9
    kernel = weights.reshape(3, 3, channels, outputs_len)[::-1, ::-1]
    grad_view = grads.reshape(outputs_len, batch_len, IMG, IMG)
    result = lax.conv_general_dilated(
        grad_view,
        kernel,
        (1, 1),
        ((1, 1), (1, 1)),
        dimension_numbers=("CNHW", "HWOI", "CNHW"),
        preferred_element_type=jnp.float32,
    )
    return result.reshape(channels, batch_len, pixels)


def maxout(pre_values, winners):
    paired = pre_values.reshape(winners.shape[0], 2, winners.shape[1], winners.shape[2])
    return jnp.where(winners == 1, paired[:, 1], paired[:, 0])


def pool_values(values, winners):
    half_side = IMG // 2
    cell_grid = values.reshape(values.shape[0], values.shape[1], half_side, 2, half_side, 2)
    pooled_sum = jnp.zeros(winners.shape, values.dtype)
    for corner in range(4):
        corner_vals = cell_grid[:, :, :, corner // 2, :, corner % 2].reshape(winners.shape)
        pooled_sum = pooled_sum + jnp.where(
            winners == corner, corner_vals, jnp.zeros_like(corner_vals)
        )
    return pooled_sum


def lamb_update(weights, grads, moment, second):
    moment_new = BETA_ONE * moment + (1.0 - BETA_ONE) * grads
    second_new = BETA_TWO * second + (1.0 - BETA_TWO) * grads * grads
    moment_hat = moment_new / (1.0 - BETA_ONE**STEP)
    second_hat = second_new / (1.0 - BETA_TWO**STEP)
    update = moment_hat / (jnp.sqrt(second_hat) + EPSILON) + DECAY * weights
    return (moment_new, second_new, update)


def on_device(
    images,
    student_master,
    regress_master,
    teacher_weight,
    student_win,
    teacher_win,
    pool_win,
    hint_mask,
    cotangent,
    mom_student,
    sq_student,
    ema_student,
    mom_regress,
    sq_regress,
    ema_regress,
):
    student_full, regress_full = (
        lax.all_gather(student_master.astype(jnp.bfloat16), "dp", axis=0, tiled=True),
        lax.all_gather(regress_master.astype(jnp.bfloat16), "dp", axis=0, tiled=True),
    )
    image_full = lax.all_gather(images, "chan", axis=0, tiled=True)
    pre_act = convolve(image_full, student_full)

    def head_pass(pre_values):
        student_vals = maxout(pre_values, student_win)
        return (student_vals, pool_values(student_vals, pool_win))

    (student_out, pooled_out), head_back = jax.vjp(head_pass, pre_act)
    out_low = student_out.astype(jnp.bfloat16)
    out_full = lax.all_gather(out_low, "chan", axis=0, tiled=True)
    regressed = convolve(out_full, regress_full)
    teacher_out = maxout(convolve(image_full, teacher_weight), teacher_win)
    mask_float = hint_mask.astype(jnp.float32)
    counts = jnp.sum(mask_float, axis=1)
    weight_map = HINT_WEIGHT * (hint_mask.shape[1] / counts)[:, None] * mask_float
    hint_grad = (weight_map[None] * (regressed - teacher_out)).astype(jnp.bfloat16)
    regress_part = filter_grad(out_full, hint_grad)
    back_hint = lax.psum_scatter(
        input_grad(hint_grad, regress_full), "chan", scatter_dimension=0, tiled=True
    )
    (pre_grad,) = head_back((back_hint, cotangent.astype(jnp.float32)))
    pre_low = pre_grad.astype(jnp.bfloat16)
    student_part = filter_grad(image_full, pre_low)
    image_grad = lax.psum_scatter(
        input_grad(pre_low, student_full), "chan", scatter_dimension=0, tiled=True
    ).astype(jnp.bfloat16)
    student_grad, regress_grad = (
        lax.psum_scatter(student_part, "dp", scatter_dimension=0, tiled=True),
        lax.psum_scatter(regress_part, "dp", scatter_dimension=0, tiled=True),
    )
    mom_s, sq_s, upd_s = lamb_update(student_master, student_grad, mom_student, sq_student)
    mom_r, sq_r, upd_r = lamb_update(regress_master, regress_grad, mom_regress, sq_regress)
    all_sums = lax.psum(
        jnp.stack(
            [
                jnp.sum(student_master * student_master),
                jnp.sum(upd_s * upd_s),
                jnp.sum(regress_master * regress_master),
                jnp.sum(upd_r * upd_r),
            ]
        ),
        ("dp", "chan"),
    )
    norm_ws = jnp.sqrt(all_sums[0])
    norm_us = jnp.sqrt(all_sums[1])
    norm_wr = jnp.sqrt(all_sums[2])
    norm_ur = jnp.sqrt(all_sums[3])
    new_student = student_master - LEARN_RATE * (norm_ws / norm_us) * upd_s
    new_regress = regress_master - LEARN_RATE * (norm_wr / norm_ur) * upd_r
    ema_s = EMA_KEEP * ema_student + (1.0 - EMA_KEEP) * new_student
    ema_r = EMA_KEEP * ema_regress + (1.0 - EMA_KEEP) * new_regress
    trust_out = jnp.stack([jnp.stack([norm_ws, norm_us]), jnp.stack([norm_wr, norm_ur])])
    return (
        pooled_out.astype(jnp.bfloat16),
        image_grad,
        new_student,
        mom_s,
        sq_s,
        ema_s,
        new_student.astype(jnp.bfloat16),
        new_regress,
        mom_r,
        sq_r,
        ema_r,
        new_regress.astype(jnp.bfloat16),
        trust_out,
    )


def solution(mesh):
    in_specs = (
        P("chan", "dp", None),
        P("dp", "chan"),
        P("dp", "chan"),
        P(None, "chan"),
        P("chan", "dp", None),
        P("chan", "dp", None),
        P("chan", "dp", None),
        P("dp", None),
        P("chan", "dp", None),
        P("dp", "chan"),
        P("dp", "chan"),
        P("dp", "chan"),
        P("dp", "chan"),
        P("dp", "chan"),
        P("dp", "chan"),
    )
    out_specs = (
        P("chan", "dp", None),
        P("chan", "dp", None),
        P("dp", "chan"),
        P("dp", "chan"),
        P("dp", "chan"),
        P("dp", "chan"),
        P("dp", "chan"),
        P("dp", "chan"),
        P("dp", "chan"),
        P("dp", "chan"),
        P("dp", "chan"),
        P("dp", "chan"),
        P(),
    )
    return jax.shard_map(
        on_device, mesh=mesh, in_specs=in_specs, out_specs=out_specs, check_vma=False
    )
```

profile of v0, /device:TPU:0, one launch (start us, length us, event | category | flops | bytes accessed | tf_op | source)
XLA Modules:
  0.0 671.7 jit_solution(12415090547203080760)
XLA Ops:
  7.2 0.7 all-gather.5.cloned.1.call-update
  8.0 0.8 convert_bitcast_fusion
  8.8 10.7 %all-gather = bf16[8,144,64]{1,2,0:T(8,128)(2,1)S(1)} all-gather(bf16[1,144,64]{1,2,0:T(8,128)(2,1)S(1)} %convert_bitcast_fusion), channel_id=1, replica_groups=mesh['dp'=8,'chan'=4] {'dp'}, dimensions={0}, use_global_device_ids=true | all-gather | bytes 165888 | tf_op jit(solution)/shard_map/all_gather | solution.py:110
  19.7 0.4 reshape.109
  20.1 73.0 %all-gather.5.cloned.1.call-done = bf16[128,16,1024]{2,1,0:T(8,128)(2,1)} async-done(((bf16[32,16,1024]{2,1,0:T(8,128)(2,1)}), bf16[128,16,1024]{2,1,0:T(8,128)(2,1)}) %all-gather.5.cloned.1.call-update) | async-done | bytes 4194320 | tf_op jit(solution)/shard_map/all_gather | solution.py:113
  93.1 7.3 %copy.82 = bf16[128,16,1024]{0,1,2:T(8,128)(2,1)} copy(bf16[128,16,1024]{2,1,0:T(8,128)(2,1)} %all-gather.5.cloned.1.call-done) | data formatting | bytes 8388608 | tf_op jit(solution)/shard_map/all_gather | solution.py:113
  100.4 13.7 %fusion.9 = f32[64,16,32,32]{0,1,3,2:T(8,128)} fusion(bf16[128,16,32,32]{0,1,3,2:T(8,128)(2,1)} %bitcast.100, bf16[3,3,128,64]{2,1,0,3:T(4,128)(2,1)S(1)} %reshape.109), kind=kOutput, calls=%fused_computation.27 | convolution fusion | flops 2316304384 | bytes 8536064 | tf_op jit(solution)/shard_map/conv_general_dilated | solution.py:23
  114.1 16.8 %copy.85 = f32[64,16,32,32]{3,2,1,0:T(8,128)} copy(f32[64,16,32,32]{0,1,3,2:T(8,128)} %fusion.9) | data formatting | bytes 8388608 | tf_op jit(solution)/shard_map/conv_general_dilated | solution.py:23
  130.9 13.8 %reshape_reshape.6 = f32[32,2,16,1024]{3,2,1,0:T(8,128)} reshape(f32[64,16,32,32]{3,2,1,0:T(8,128)} %copy.85) | data formatting | bytes 8388608 | tf_op jit(solution)/shard_map/jvp()/reshape;reshape | solution.py:67
  144.7 4.9 fusion.21
  149.7 9.5 %all-gather.1 = bf16[8,144,48]{1,2,0:T(8,128)(2,1)S(1)} all-gather(bf16[1,144,48]{1,2,0:T(8,128)(2,1)S(1)} %convert_bitcast_fusion.1), channel_id=1, replica_groups=mesh['dp'=8,'chan'=4] {'dp'}, dimensions={0}, use_global_device_ids=true | all-gather | bytes 124416 | tf_op jit(solution)/shard_map/all_gather | solution.py:111
  159.3 0.3 reshape.112
  159.9 13.7 %fusion.5 = f32[96,16,32,32]{0,1,3,2:T(8,128)} fusion(bf16[128,16,32,32]{0,1,3,2:T(8,128)(2,1)} %bitcast.101, bf16[3,3,128,96]{2,1,0,3:T(4,128)(2,1)S(1)} %reshape.114), kind=kOutput, calls=%fused_computation.23 | convolution fusion | flops 3474456576 | bytes 10706944 | tf_op jit(solution)/shard_map/conv_general_dilated | solution.py:23
  173.6 21.5 %copy.99 = f32[96,16,32,32]{3,2,1,0:T(8,128)} copy(f32[96,16,32,32]{0,1,3,2:T(8,128)} %fusion.5) | data formatting | bytes 12582912 | tf_op jit(solution)/shard_map/conv_general_dilated | solution.py:23
  195.1 20.0 %reshape_reshape.7 = f32[48,2,16,1024]{3,2,1,0:T(8,128)} reshape(f32[96,16,32,32]{3,2,1,0:T(8,128)} %copy.99) | data formatting | bytes 12582912 | tf_op jit(solution)/shard_map/reshape;reshape | solution.py:67
  215.0 14.1 %all-gather.7.cloned.1.call-done = bf16[128,16,1024]{2,1,0:T(8,128)(2,1)} async-done(((bf16[32,16,1024]{2,1,0:T(8,128)(2,1)}), bf16[128,16,1024]{2,1,0:T(8,128)(2,1)}) %all-gather.7.cloned.1.call-update) | async-done | bytes 4194320 | tf_op jit(solution)/shard_map/all_gather | solution.py:122
  229.1 7.3 %copy.95 = bf16[128,16,1024]{0,1,2:T(8,128)(2,1)} copy(bf16[128,16,1024]{2,1,0:T(8,128)(2,1)} %all-gather.7.cloned.1.call-done) | data formatting | bytes 8388608 | tf_op jit(solution)/shard_map/all_gather | solution.py:122
  236.4 14.1 %fusion.13 = f32[48,16,32,32]{0,1,3,2:T(8,128)} fusion(bf16[128,16,32,32]{0,1,3,2:T(8,128)(2,1)} %bitcast.103, bf16[3,3,128,48]{2,1,0,3:T(4,128)(2,1)S(1)} %reshape.112), kind=kOutput, calls=%fused_computation.32 | convolution fusion | flops 1737228288 | bytes 7450624 | tf_op jit(solution)/shard_map/conv_general_dilated | solution.py:23
  250.5 6.1 copy.101
  256.6 6.4 fusion.3
  263.0 7.9 %copy.121 = bf16[48,16,1024]{0,1,2:T(8,128)(2,1)} copy(bf16[48,16,1024]{2,1,0:T(8,128)(2,1)} %fusion.3) | data formatting | bytes 3145728 | tf_op jit(solution)/shard_map/reshape | solution.py:54
  271.0 13.2 %fusion.11 = f32[128,16,32,32]{0,1,3,2:T(8,128)} fusion(bf16[48,16,32,32]{0,1,3,2:T(8,128)(2,1)} %bitcast.105, bf16[3,3,128,48]{2,1,0,3:T(4,128)(2,1)S(1)} %reshape.112), kind=kOutput, calls=%fused_computation.30 | convolution fusion | flops 1737228288 | bytes 10072064 | tf_op jit(solution)/shard_map/conv_general_dilated | solution.py:55
  284.2 8.8 %copy.104 = f32[128,16,1024]{2,1,0:T(8,128)} copy(f32[128,16,1024]{0,1,2:T(8,128)} %bitcast.90) | data formatting | bytes 16777216 | tf_op jit(solution)/shard_map/reshape | solution.py:63
  293.1 0.9 copy-done.10
  294.0 0.5 copy.105
  294.5 1.7 copy.81
  296.1 3.0 convert_select_fusion
  299.1 1.1 pad_add_fusion
  300.2 8.1 %copy.106 = f32[32,16,16,2,16,2]{0,1,5,4,3,2:T(8,128)} copy(f32[32,16,16,2,16,2]{0,4,2,1,5,3:T(8,128)S(1)} %pad_add_fusion) | data formatting | bytes 4194304 | tf_op jit(solution)/shard_map/transpose(jvp())/add_any | solution.py:76
  308.3 5.8 copy.107
  314.2 18.0 %fusion.26 = f32[3,3,128,48]{3,2,1,0:T(8,128)} fusion(bf16[128,16,32,32]{0,1,3,2:T(8,128)(2,1)} %bitcast.104, bf16[48,16,32,32]{0,1,3,2:T(8,128)(2,1)} %bitcast.106), kind=kOutput, calls=%fused_computation.64 | convolution fusion | flops 1737228288 | bytes 5988352
  332.2 104.0 %reduce-scatter.9.cloned.1.call-done = f32[32,16,1024]{2,1,0:T(8,128)} async-done(((f32[128,16,1024]{2,1,0:T(8,128)}), f32[32,16,1024]{2,1,0:T(8,128)}) %reduce-scatter.9.cloned.1.call-update) | async-done | bytes 2097168 | tf_op jit(solution)/shard_map/reduce_scatter | solution.py:130
  436.2 2.3 select_bitcast_fusion.1
  438.6 0.3 add_convert_fusion
  439.1 8.4 %convert_element_type.45 = bf16[64,16,32,32]{3,2,1,0:T(8,128)(2,1)} reshape(bf16[32,2,16,1024]{3,2,1,0:T(8,128)(2,1)S(1)} %copy.108) | data formatting | bytes 4194304 | tf_op jit(solution)/shard_map/convert_element_type | solution.py:134
  447.5 13.4 %copy.109 = bf16[64,16,32,32]{0,1,3,2:T(8,128)(2,1)} copy(bf16[64,16,32,32]{3,2,1,0:T(8,128)(2,1)} %convert_element_type.45) | data formatting | bytes 4194304 | tf_op jit(solution)/shard_map/convert_element_type | solution.py:134
  460.9 17.7 %fusion.25 = f32[3,3,128,64]{3,2,1,0:T(8,128)} fusion(bf16[128,16,32,32]{0,1,3,2:T(8,128)(2,1)} %bitcast.102, bf16[64,16,32,32]{0,1,3,2:T(8,128)(2,1)} %copy.109), kind=kOutput, calls=%fused_computation.63 | convolution fusion | flops 2316304384 | bytes 6586368
  478.7 0.2 reduce-scatter.11.cloned.1.call-start
  478.9 11.1 %fusion.7 = f32[128,16,32,32]{0,1,3,2:T(8,128)} fusion(bf16[64,16,32,32]{0,1,3,2:T(8,128)(2,1)} %copy.109, bf16[3,3,128,64]{2,1,0,3:T(4,128)(2,1)S(1)} %copy-done.17), kind=kOutput, calls=%fused_computation.25 | convolution fusion | flops 2316304384 | bytes 10633216 | tf_op jit(solution)/shard_map/conv_general_dilated | solution.py:55
  490.0 9.0 %copy.111 = f32[128,16,1024]{2,1,0:T(8,128)} copy(f32[128,16,1024]{0,1,2:T(8,128)} %bitcast.89) | data formatting | bytes 16777216 | tf_op jit(solution)/shard_map/reshape | solution.py:63
  499.1 1.6 copy-done
  500.7 6.5 copy.87
  507.2 4.1 fusion.23
  511.4 0.7 copy.88
  512.0 0.7 copy.94
  512.7 0.7 copy.92
  513.5 0.7 copy.90
  514.1 0.3 copy-done.3
  515.0 1.3 add_convert_fusion.1
  516.3 1.0 copy.120
  517.3 0.7 multiply_reduce_fusion.3
  518.0 1.0 copy.118
  519.0 0.7 multiply_reduce_fusion.1
  519.7 2.7 pad_maximum_fusion.1
  522.3 1.2 copy.116
  523.5 45.0 %psum.7 = f32[4]{0:T(128)S(1)} all-reduce(f32[4]{0:T(128)S(1)} %pad_maximum_fusion.1), channel_id=1, replica_groups=mesh['dp'=8,'chan'=4] {'dp','chan'}, use_global_device_ids=true, to_apply=%region_9.10 | all-reduce | flops 4 | bytes 32 | tf_op jit(solution)/shard_map/psum | solution.py:145
  568.6 0.6 fusion.24
  572.1 0.6 pad_maximum_fusion
  572.7 0.6 fusion.17
  573.3 0.6 multiply_add_fusion.3
  573.9 0.7 fusion.18
  574.6 0.6 multiply_add_fusion
  575.3 86.6 %reduce-scatter.11.cloned.1.call-done = f32[32,16,1024]{2,1,0:T(8,128)} async-done(((f32[128,16,1024]{2,1,0:T(8,128)}), f32[32,16,1024]{2,1,0:T(8,128)}) %reduce-scatter.11.cloned.1.call-update) | async-done | bytes 2097168 | tf_op jit(solution)/shard_map/reduce_scatter | solution.py:136
  661.8 2.7 convert_element_type.46
  (72 shorter events, 1.6 us)
Async XLA Ops:
  7.2 85.9 %all-gather.5.cloned.1.call-start = ((), (), s32[]{:S(2)}) async-start(), calls=%async_computation.4 | async-start | bytes 5242880 | tf_op jit(solution)/shard_map/all_gather | solution.py:113
  7.9 221.2 %all-gather.7.cloned.1.call-start = ((), (), s32[]{:S(2)}) async-start(), calls=%async_computation.5 | async-start | bytes 5242880 | tf_op jit(solution)/shard_map/all_gather | solution.py:122
  20.1 80.3 %copy-start.16 = (bf16[3,3,128,64]{2,1,0,3:T(4,128)(2,1)}, bf16[3,3,128,64]{2,1,0,3:T(4,128)(2,1)S(1)}, u32[]{:S(2)}) copy-start(bf16[3,3,128,64]{2,1,0,3:T(4,128)(2,1)S(1)} %reshape.109) | copy-start | bytes 442372
  130.9 13.8 %copy-start.1 = (s32[32,16,1024]{2,1,0:T(8,128)S(1)}, s32[32,16,1024]{2,1,0:T(8,128)}, u32[]{:S(2)}) copy-start(s32[32,16,1024]{2,1,0:T(8,128)} %param.19) | copy-start | bytes 6291460
  144.7 5.0 copy-start.8
  144.7 14.9 %copy-start.15 = (bf16[1152,96]{0,1:T(8,128)(2,1)S(1)}, bf16[1152,96]{0,1:T(8,128)(2,1)}, u32[]{:S(2)}) copy-start(bf16[1152,96]{0,1:T(8,128)(2,1)} %param.18) | copy-start | bytes 663556
  144.7 15.0 %copy-start.11 = (s32[16,1024]{1,0:T(8,128)S(1)}, s32[16,1024]{1,0:T(8,128)}, u32[]{:S(2)}) copy-start(s32[16,1024]{1,0:T(8,128)} %param.22) | copy-start | bytes 196612
  149.7 286.5 %reduce-scatter.9.cloned.1.call-start = ((), (), s32[]{:S(2)}) async-start(), calls=%async_computation.6 | async-start | bytes 10485760 | tf_op jit(solution)/shard_map/reduce_scatter | solution.py:130
  293.0 0.9 copy-start.10
  293.0 223.2 %reduce-scatter.15.cloned.1.call-start = ((), (), s32[]{:S(2)}) async-start(), calls=%async_computation.9 | async-start | bytes 663552
  314.2 122.0 %copy-start.2 = (pred[32,16,1024]{2,1,0:T(8,128)(4,1)S(1)}, pred[32,16,1024]{2,1,0:T(8,128)(4,1)}, u32[]{:S(2)}) copy-start(pred[32,16,1024]{2,1,0:T(8,128)(4,1)} %get-tuple-element.61) | copy-start | bytes 1572868
  332.2 185.8 %reduce-scatter.13.cloned.1.call-start = ((), (), s32[]{:S(2)}) async-start(), calls=%async_computation.8 | async-start | bytes 663552
  460.9 18.0 %copy-start.17 = (bf16[3,3,128,64]{2,1,0,3:T(4,128)(2,1)S(1)}, bf16[3,3,128,64]{2,1,0,3:T(4,128)(2,1)}, u32[]{:S(2)}) copy-start(bf16[3,3,128,64]{2,1,0,3:T(4,128)(2,1)} %copy-done.16) | copy-start | bytes 442372
  478.7 183.1 %reduce-scatter.11.cloned.1.call-start = ((), (), s32[]{:S(2)}) async-start(), calls=%async_computation.7 | async-start | bytes 10485760 | tf_op jit(solution)/shard_map/reduce_scatter | solution.py:136
  499.1 1.6 copy-start
  513.4 1.0 copy-start.3
  513.4 1.2 copy-start.4
  513.4 1.4 copy-start.5
  513.4 1.5 copy-start.6
  514.9 2.3 copy-start.9
  514.9 2.3 copy-start.24
  514.9 2.3 copy-start.25
  515.0 4.0 copy-start.7
  515.0 4.0 copy-start.22
  515.0 4.0 copy-start.23
  515.0 58.3 %copy-start.26 = (f32[144,48]{0,1:T(8,128)S(1)}, f32[144,48]{0,1:T(8,128)}, u32[]{:S(2)}) copy-start(f32[144,48]{0,1:T(8,128)} %param.29) | copy-start | bytes 82948
  515.0 59.6 %copy-start.21 = (f32[144,64]{0,1:T(8,128)S(1)}, f32[144,64]{0,1:T(8,128)}, u32[]{:S(2)}) copy-start(f32[144,64]{0,1:T(8,128)} %param.26) | copy-start | bytes 110596
  517.9 146.6 %copy-start.18 = (f32[144,48]{0,1:T(8,128)}, f32[144,48]{0,1:T(8,128)S(1)}, u32[]{:S(2)}) copy-start(f32[144,48]{0,1:T(8,128)S(1)} %get-tuple-element.49) | copy-start | bytes 82948
  517.9 146.6 %copy-start.19 = (f32[144,48]{0,1:T(8,128)}, f32[144,48]{0,1:T(8,128)S(1)}, u32[]{:S(2)}) copy-start(f32[144,48]{0,1:T(8,128)S(1)} %get-tuple-element.50) | copy-start | bytes 82948
  519.7 144.9 %copy-start.13 = (f32[144,64]{0,1:T(8,128)}, f32[144,64]{0,1:T(8,128)S(1)}, u32[]{:S(2)}) copy-start(f32[144,64]{0,1:T(8,128)S(1)} %get-tuple-element.47) | copy-start | bytes 110596
  519.7 144.9 %copy-start.14 = (f32[144,64]{0,1:T(8,128)}, f32[144,64]{0,1:T(8,128)S(1)}, u32[]{:S(2)}) copy-start(f32[144,64]{0,1:T(8,128)S(1)} %get-tuple-element.48) | copy-start | bytes 110596
  573.3 91.3 %copy-start.20 = (f32[144,48]{0,1:T(8,128)}, f32[144,48]{0,1:T(8,128)S(1)}, u32[]{:S(2)}) copy-start(f32[144,48]{0,1:T(8,128)S(1)} %get-tuple-element.44) | copy-start | bytes 82948
  574.6 90.0 %copy-start.12 = (f32[144,64]{0,1:T(8,128)}, f32[144,64]{0,1:T(8,128)S(1)}, u32[]{:S(2)}) copy-start(f32[144,64]{0,1:T(8,128)S(1)} %get-tuple-element.46) | copy-start | bytes 110596
Sparse Core Ops, SparseCore 0:
  9.6 83.4 all-gather.4
  149.8 79.2 all-gather.6
  293.2 143.0 reduce-scatter.8
  439.2 35.1 reduce-scatter.14
  478.8 35.1 reduce-scatter.12
  516.2 145.5 reduce-scatter.10
where the time goes:
time: 682 us; the launch traced here: 672 us
  waiting for transfers between devices  278 us (41%)
  local copies, waits for them, and re-layouts  178 us (26%)
  matrix products  102 us (15%)
  blocking collectives  65.3 us (10%)
  other arithmetic  30.4 us (4%)
  between operations  17.6 us (3%)
    reduce_scatter x1, waiting for transfers between devices, on_device(): lax.psum_scatter(input_grad(hint_grad, regress_full), 'chan', scatter_dim...  104 us
    reduce_scatter x1, waiting for transfers between devices, on_device(): lax.psum_scatter(input_grad(pre_low, student_full), 'chan', scatter_dimen...  86.6 us
    all_gather x1, waiting for transfers between devices, on_device(): image_full = lax.all_gather(images, 'chan', axis=0, tiled=True)  73 us
    psum x1, blocking collectives, on_device(): lax.psum(jnp.stack([jnp.sum(student_master * student_master), jnp.sum(upd...  45 us
    conv_general_dilated x3, matrix products, convolve(): lax.conv_general_dilated(left_view, kernel, (1, 1), ((1, 1), (1, 1)), dim...  41.5 us
    conv_general_dilated x2, local copies, waits for them, and re-layouts, convolve(): lax.conv_general_dilated(left_view, kernel, (1, 1), ((1, 1), (1, 1)), dim...  38.2 us
    unnamed x2, matrix products  35.7 us
    another operation x2, local copies, waits for them, and re-layouts, maxout(): pre_values.reshape(winners.shape[0], 2, winners.shape[1], winners.shape[2])  33.8 us
  transfers between devices with their start and end apart: 6, of which 4 were waited for; matrix products, arithmetic and copies ran while one was open for 27% of the time, Pallas kernels for 0%

commit v1 on v0

v1 whole, which is shorter than its diff:
```python
import functools

import jax
import jax.numpy as jnp
from jax import lax
from jax.experimental import pallas as pl
from jax.experimental.pallas import tpu as pltpu
from jax.sharding import PartitionSpec as P

IMG = 32
STEP = 10
HINT_WEIGHT = 0.1
LEARN_RATE = 0.5
BETA_ONE = 0.9
BETA_TWO = 0.999
EPSILON = 1e-06
DECAY = 0.01
EMA_KEEP = 0.75

MESH = pl.DeviceIdType.MESH
F32 = jnp.float32
BF16 = jnp.bfloat16
CHUNK = 256
LANES = 128


def dot(left, right):
    return jnp.dot(left, right, preferred_element_type=F32)


def dot_nt(left, right):
    return lax.dot_general(left, right, (((1,), (1,)), ((), ())), preferred_element_type=F32)


def layer_kernel(
    size,
    images,
    swin,
    twin,
    pwin,
    cot,
    mask,
    w_in,
    w_reg,
    w_reg_back,
    w_in_back,
    pool_out,
    grad_out,
    sgrad,
    rgrad,
    raw,
    raw_cot,
    wide,
    swin_wide,
    twin_wide,
    pwin_wide,
    cot_wide,
    load_sem,
    send,
    send_pool,
    held,
    held_pool,
    low_part,
    pool_part,
    edge,
    up,
    x_cols,
    o_cols,
    h_cols,
    p_cols,
    out_low,
    pool_back,
    hint,
    pre_grad,
    in_send,
    in_recv,
    pool_in_send,
    pool_in_recv,
    own_sem,
    out_send,
    out_recv,
    pool_out_send,
    pool_out_recv,
    own_out_sem,
):
    n, batch, cl, tl = size["n"], size["batch"], size["cl"], size["tl"]
    slots = batch // n
    chans, touts = n * cl, n * tl
    pixels = IMG * IMG
    cells = pixels // 4
    me = lax.axis_index("chan")

    barrier = pltpu.get_barrier_semaphore()
    for step in range(1, n):
        pl.semaphore_signal(
            barrier, inc=1, device_id={"chan": lax.rem(me + step, n)}, device_id_type=MESH
        )
    pl.semaphore_wait(barrier, n - 1)

    loads = [
        pltpu.make_async_copy(images, raw, load_sem.at[0]),
        pltpu.make_async_copy(cot, raw_cot, load_sem.at[1]),
    ]
    for src, dst in ((swin, swin_wide), (twin, twin_wide), (pwin, pwin_wide)):
        for j in range(dst.shape[0]):
            loads.append(
                pltpu.make_async_copy(
                    src.at[:, pl.ds(j * LANES, LANES)], dst.at[j], load_sem.at[len(loads)]
                )
            )
    for copy in loads:
        copy.start()
    for copy in loads:
        copy.wait()
    for j in range(wide.shape[0]):
        wide[j] = raw[:, j * LANES : (j + 1) * LANES].astype(F32)
    for j in range(cot_wide.shape[0]):
        cot_wide[j] = raw_cot[:, j * LANES : (j + 1) * LANES].astype(F32)

    def in_copies(slot, step):
        to = lax.rem(me + step, n)
        return (
            pltpu.make_async_remote_copy(
                send.at[slot, to],
                held.at[slot, me],
                in_send.at[slot, step],
                in_recv.at[slot, step],
                device_id={"chan": to},
                device_id_type=MESH,
            ),
            pltpu.make_async_remote_copy(
                send_pool.at[slot, to],
                held_pool.at[slot, me],
                pool_in_send.at[slot, step],
                pool_in_recv.at[slot, step],
                device_id={"chan": to},
                device_id_type=MESH,
            ),
        )

    def own_copies(slot):
        return (
            pltpu.make_async_copy(send.at[slot, me], held.at[slot, me], own_sem.at[slot, 0]),
            pltpu.make_async_copy(
                send_pool.at[slot, me], held_pool.at[slot, me], own_sem.at[slot, 1]
            ),
        )

    def out_copies(slot, step):
        to = lax.rem(me + step, n)
        return (
            pltpu.make_async_remote_copy(
                low_part.at[slot, pl.ds(pl.multiple_of(to * cl, cl), cl)],
                grad_out.at[me * slots + slot],
                out_send.at[slot, step],
                out_recv.at[slot, step],
                device_id={"chan": to},
                device_id_type=MESH,
            ),
            pltpu.make_async_remote_copy(
                pool_part.at[slot, pl.ds(pl.multiple_of(to * cl, cl), cl)],
                pool_out.at[me * slots + slot],
                pool_out_send.at[slot, step],
                pool_out_recv.at[slot, step],
                device_id={"chan": to},
                device_id_type=MESH,
            ),
        )

    def own_out(slot):
        mine = pl.ds(pl.multiple_of(me * cl, cl), cl)
        return (
            pltpu.make_async_copy(
                low_part.at[slot, mine], grad_out.at[me * slots + slot], own_out_sem.at[slot, 0]
            ),
            pltpu.make_async_copy(
                pool_part.at[slot, mine], pool_out.at[me * slots + slot], own_out_sem.at[slot, 1]
            ),
        )

    def prepare(slot, carry):
        for to in range(n):
            row = to * slots + slot
            for src, dst, first, rows in (
                (wide, send, 0, cl),
                (swin_wide, send, cl, cl),
                (twin_wide, send, 2 * cl, tl),
                (pwin_wide, send_pool, 0, cl),
                (cot_wide, send_pool, cl, cl),
            ):
                for j in range(src.shape[0]):
                    dst[slot, to, first : first + rows, j * LANES : (j + 1) * LANES] = (
                        src[j, pl.ds(row, rows, stride=batch), :].astype(F32).astype(BF16)
                    )
        for step in range(1, n):
            for copy in in_copies(slot, step):
                copy.start()
        for copy in own_copies(slot):
            copy.start()
        return carry

    lax.fori_loop(0, slots, prepare, 0)

    lane = lax.broadcasted_iota(jnp.int32, (16, pixels), 1)
    row_of, col_of = lane // IMG, lane % IMG
    for which, bad in enumerate((row_of == 0, row_of == IMG - 1, col_of == 0, col_of == IMG - 1)):
        edge[which] = jnp.where(bad, 0.0, 1.0).astype(BF16)
    cell = lax.broadcasted_iota(jnp.int32, (cells, pixels), 0)
    spot = lax.broadcasted_iota(jnp.int32, (cells, pixels), 1)
    home = (spot // (2 * IMG)) * (IMG // 2) + (spot % IMG) // 2
    up[...] = jnp.where(cell == home, 1.0, 0.0).astype(BF16)
    sgrad[...] = jnp.zeros_like(sgrad)
    rgrad[...] = jnp.zeros_like(rgrad)

    def columns(load, rows, dst):
        def group(g, carry):
            first = pl.multiple_of(g * 16, 16)
            base = load(first)
            for ky in range(3):
                if ky == 1:
                    moved = base
                else:
                    moved = pltpu.roll(base, (pixels - IMG * (ky - 1)) % pixels, 1)
                    moved = moved * edge[0 if ky == 0 else 1]
                for kx in range(3):
                    if kx == 1:
                        tap = moved
                    else:
                        tap = pltpu.roll(moved, (pixels - (kx - 1)) % pixels, 1)
                        tap = tap * edge[2 if kx == 0 else 3]
                    dst[pl.ds((3 * ky + kx) * rows + first, 16), :] = tap
            return carry

        lax.fori_loop(0, rows // 16, group, 0)

    def chunks(body):
        def one(c, carry):
            body(pl.ds(pl.multiple_of(c * CHUNK, CHUNK), CHUNK))
            return carry

        lax.fori_loop(0, pixels // CHUNK, one, 0)

    def corner_of(here):
        at = lax.broadcasted_iota(jnp.int32, (1, CHUNK), 1)
        return (2 * ((at // IMG) % 2) + at % 2).astype(F32)

    def image(slot, carry):
        for step in range(1, n):
            for copy in in_copies(slot, step):
                copy.wait_recv()
        for copy in own_copies(slot):
            copy.wait()

        def image_rows(first):
            return held[slot, first // cl, pl.ds(pl.multiple_of(first % cl, 16), 16), :]

        columns(image_rows, chans, x_cols)
        pool_part[slot] = jnp.zeros((chans, cells), BF16)

        def head(here):
            pre = dot(w_in[0 : 2 * chans, :], x_cols[:, here])
            pick = held[slot, :, cl : 2 * cl, here].reshape(chans, CHUNK).astype(F32)
            value = jnp.where(pick > 0.5, pre[chans:], pre[:chans]).astype(BF16)
            out_low[:, here] = value
            cell_win = held_pool[slot, :, 0:cl, :].reshape(chans, cells)
            cell_cot = held_pool[slot, :, cl : 2 * cl, :].reshape(chans, cells)
            chosen = dot(cell_win, up[:, here]) == corner_of(here)
            spread = dot(cell_cot, up[:, here])
            pool_back[:, here] = jnp.where(chosen, spread, 0.0).astype(BF16)
            kept = jnp.where(chosen, value.astype(F32), 0.0).astype(BF16)
            part = dot_nt(kept, up[:, here])
            pool_part[slot] = (pool_part[slot].astype(F32) + part).astype(BF16)

        chunks(head)
        columns(lambda first: out_low[pl.ds(first, 16), :], chans, o_cols)

        spot_mask = mask[pl.ds(me * slots + slot, 1), :].astype(F32)
        count = jnp.sum(spot_mask, axis=1, keepdims=True)
        scale = HINT_WEIGHT * (pixels / count)

        def hints(here):
            teach = dot(w_in[2 * chans :, :], x_cols[:, here])
            pick = held[slot, :, 2 * cl :, here].reshape(touts, CHUNK).astype(F32)
            target = jnp.where(pick > 0.5, teach[touts:], teach[:touts])
            guess = dot(w_reg[...], o_cols[:, here])
            weight = scale * mask[pl.ds(me * slots + slot, 1), here].astype(F32)
            hint[:, here] = (weight * (guess - target)).astype(BF16)

        chunks(hints)
        columns(lambda first: hint[pl.ds(first, 16), :], hint.shape[0], h_cols)
        rgrad[...] += dot_nt(o_cols[...], hint[...])

        def back(here):
            total = dot(w_reg_back[...], h_cols[:, here]) + pool_back[:, here].astype(F32)
            pick = held[slot, :, cl : 2 * cl, here].reshape(chans, CHUNK).astype(F32) > 0.5
            pre_grad[0:chans, here] = jnp.where(pick, 0.0, total).astype(BF16)
            pre_grad[chans:, here] = jnp.where(pick, total, 0.0).astype(BF16)

        chunks(back)
        columns(lambda first: pre_grad[pl.ds(first, 16), :], 2 * chans, p_cols)
        sgrad[...] += dot_nt(x_cols[...], pre_grad[...])

        def image_back(here):
            low_part[slot, :, here] = dot(w_in_back[...], p_cols[:, here]).astype(BF16)

        chunks(image_back)
        for step in range(1, n):
            for copy in out_copies(slot, step):
                copy.start()
        for copy in own_out(slot):
            copy.start()
        return carry

    lax.fori_loop(0, slots, image, 0)

    def finish(slot, carry):
        for step in range(1, n):
            for copy in in_copies(slot, step):
                copy.wait_send()
            for copy in out_copies(slot, step):
                copy.wait()
        for copy in own_out(slot):
            copy.wait()
        return carry

    lax.fori_loop(0, slots, finish, 0)


def layer_pass(n, images, swin, twin, pwin, cot, mask, w_in, w_reg, w_reg_back, w_in_back):
    cl, batch, pixels = images.shape
    tl = twin.shape[0]
    cells = pwin.shape[2]
    slots = batch // n
    chans, touts = n * cl, n * tl
    regs = w_reg.shape[0]
    size = {"n": n, "batch": batch, "cl": cl, "tl": tl}
    vmem = pl.BlockSpec(memory_space=pltpu.VMEM)
    flat = lambda a: a.reshape(a.shape[0] * a.shape[1], a.shape[2])
    flops = 2 * slots * pixels * 9 * chans * (3 * 2 * chans + 2 * touts + 3 * regs)
    return pl.pallas_call(
        functools.partial(layer_kernel, size),
        out_shape=[
            jax.ShapeDtypeStruct((batch, cl, cells), BF16),
            jax.ShapeDtypeStruct((batch, cl, pixels), BF16),
            jax.ShapeDtypeStruct((9 * chans, 2 * chans), F32),
            jax.ShapeDtypeStruct((9 * chans, regs), F32),
        ],
        in_specs=[pl.BlockSpec(memory_space=pl.ANY)] * 5 + [vmem] * 5,
        out_specs=[vmem] * 4,
        scratch_shapes=[
            pltpu.VMEM((cl * batch, pixels), BF16),
            pltpu.VMEM((cl * batch, cells), BF16),
            pltpu.VMEM((pixels // LANES, cl * batch, LANES), F32),
            pltpu.VMEM((pixels // LANES, cl * batch, LANES), jnp.int32),
            pltpu.VMEM((pixels // LANES, tl * batch, LANES), jnp.int32),
            pltpu.VMEM((cells // LANES, cl * batch, LANES), jnp.int32),
            pltpu.VMEM((cells // LANES, cl * batch, LANES), F32),
            pltpu.SemaphoreType.DMA((2 + 2 * (pixels // LANES) + cells // LANES,)),
            pltpu.VMEM((slots, n, 2 * cl + tl, pixels), BF16),
            pltpu.VMEM((slots, n, 2 * cl, cells), BF16),
            pltpu.VMEM((slots, n, 2 * cl + tl, pixels), BF16),
            pltpu.VMEM((slots, n, 2 * cl, cells), BF16),
            pltpu.VMEM((slots, chans, pixels), BF16),
            pltpu.VMEM((slots, chans, cells), BF16),
            pltpu.VMEM((4, 16, pixels), BF16),
            pltpu.VMEM((cells, pixels), BF16),
            pltpu.VMEM((9 * chans, pixels), BF16),
            pltpu.VMEM((9 * chans, pixels), BF16),
            pltpu.VMEM((9 * regs, pixels), BF16),
            pltpu.VMEM((9 * 2 * chans, pixels), BF16),
            pltpu.VMEM((chans, pixels), BF16),
            pltpu.VMEM((chans, pixels), BF16),
            pltpu.VMEM((regs, pixels), BF16),
            pltpu.VMEM((2 * chans, pixels), BF16),
            pltpu.SemaphoreType.DMA((slots, n)),
            pltpu.SemaphoreType.DMA((slots, n)),
            pltpu.SemaphoreType.DMA((slots, n)),
            pltpu.SemaphoreType.DMA((slots, n)),
            pltpu.SemaphoreType.DMA((slots, 2)),
            pltpu.SemaphoreType.DMA((slots, n)),
            pltpu.SemaphoreType.DMA((slots, n)),
            pltpu.SemaphoreType.DMA((slots, n)),
            pltpu.SemaphoreType.DMA((slots, n)),
            pltpu.SemaphoreType.DMA((slots, 2)),
        ],
        compiler_params=pltpu.CompilerParams(
            collective_id=0, has_side_effects=True, vmem_limit_bytes=56 << 20
        ),
        cost_estimate=pl.CostEstimate(flops=flops, bytes_accessed=16 << 20, transcendentals=0),
        name="layer",
    )(
        flat(images),
        flat(swin),
        flat(twin),
        flat(pwin),
        flat(cot),
        mask,
        w_in,
        w_reg,
        w_reg_back,
        w_in_back,
    )


def split_pieces(weights):
    rows, cols = weights.shape
    return weights.reshape(rows, cols // 2, 2).transpose(2, 1, 0).reshape(cols, rows)


def back_weights(weights, outs):
    channels = weights.shape[0] // 9
    taps = weights.reshape(9, channels, outs)[::-1]
    return taps.transpose(1, 0, 2).reshape(channels, 9 * outs)


def lamb_update(weights, grads, moment, second):
    moment_new = BETA_ONE * moment + (1.0 - BETA_ONE) * grads
    second_new = BETA_TWO * second + (1.0 - BETA_TWO) * grads * grads
    moment_hat = moment_new / (1.0 - BETA_ONE**STEP)
    second_hat = second_new / (1.0 - BETA_TWO**STEP)
    update = moment_hat / (jnp.sqrt(second_hat) + EPSILON) + DECAY * weights
    return (moment_new, second_new, update)


def on_device(
    n,
    images,
    student_master,
    regress_master,
    teacher_weight,
    student_win,
    teacher_win,
    pool_win,
    hint_mask,
    cotangent,
    mom_student,
    sq_student,
    ema_student,
    mom_regress,
    sq_regress,
    ema_regress,
):
    student_full = lax.all_gather(student_master.astype(BF16), "dp", axis=0, tiled=True)
    student_full = lax.all_gather(student_full, "chan", axis=1, tiled=True)
    regress_full = lax.all_gather(regress_master.astype(BF16), "dp", axis=0, tiled=True)
    regress_full = lax.all_gather(regress_full, "chan", axis=1, tiled=True)
    teacher_full = lax.all_gather(teacher_weight, "chan", axis=1, tiled=True)
    souts = student_full.shape[1]
    regs = regress_full.shape[1]
    student_rows = split_pieces(student_full)
    w_in = jnp.concatenate([student_rows, split_pieces(teacher_full)], axis=0)
    pooled, image_grad, student_part, regress_part = layer_pass(
        n,
        images,
        student_win,
        teacher_win,
        pool_win,
        cotangent,
        hint_mask,
        w_in,
        regress_full.T,
        back_weights(regress_full, regs),
        back_weights(student_rows.T, souts),
    )
    half = souts // 2
    student_part = student_part.reshape(-1, 2, half).transpose(0, 2, 1).reshape(-1, souts)
    student_grad = lax.psum_scatter(student_part, "dp", scatter_dimension=0, tiled=True)
    student_grad = lax.psum_scatter(student_grad, "chan", scatter_dimension=1, tiled=True)
    regress_grad = lax.psum_scatter(regress_part, "dp", scatter_dimension=0, tiled=True)
    regress_grad = lax.psum_scatter(regress_grad, "chan", scatter_dimension=1, tiled=True)
    mom_s, sq_s, upd_s = lamb_update(student_master, student_grad, mom_student, sq_student)
    mom_r, sq_r, upd_r = lamb_update(regress_master, regress_grad, mom_regress, sq_regress)
    all_sums = lax.psum(
        jnp.stack(
            [
                jnp.sum(student_master * student_master),
                jnp.sum(upd_s * upd_s),
                jnp.sum(regress_master * regress_master),
                jnp.sum(upd_r * upd_r),
            ]
        ),
        ("dp", "chan"),
    )
    norms = jnp.sqrt(all_sums)
    new_student = student_master - LEARN_RATE * (norms[0] / norms[1]) * upd_s
    new_regress = regress_master - LEARN_RATE * (norms[2] / norms[3]) * upd_r
    ema_s = EMA_KEEP * ema_student + (1.0 - EMA_KEEP) * new_student
    ema_r = EMA_KEEP * ema_regress + (1.0 - EMA_KEEP) * new_regress
    return (
        pooled.transpose(1, 0, 2),
        image_grad.transpose(1, 0, 2),
        new_student,
        mom_s,
        sq_s,
        ema_s,
        new_student.astype(BF16),
        new_regress,
        mom_r,
        sq_r,
        ema_r,
        new_regress.astype(BF16),
        norms.reshape(2, 2),
    )


def solution(mesh):
    acts = P("chan", "dp", None)
    rows = P("dp", "chan")
    in_specs = (
        (acts, rows, rows, P(None, "chan"))
        + (acts, acts, acts, P("dp", None), acts)
        + (rows,) * 6
    )
    out_specs = (acts, acts) + (rows,) * 10 + (P(),)
    return jax.shard_map(
        functools.partial(on_device, mesh.shape["chan"]),
        mesh=mesh,
        in_specs=in_specs,
        out_specs=out_specs,
        check_vma=False,
    )
```

time: 682 us -> 400 us (0.59); the launches traced: 672 us -> 399 us
  waiting for transfers between devices: 278 us -> 108 us
  local copies, waits for them, and re-layouts: 178 us -> 16.4 us
  Pallas kernels: 0 us -> 138 us
  matrix products: 102 us -> 0 us
  blocking collectives: 65.3 us -> 109 us
  other arithmetic: 30.4 us -> 11.2 us
    reduce_scatter x2, waiting for transfers between devices: 191 us -> 50 us  [the longest x1 31 us: on_device(): lax.psum_scatter(regress_part, 'dp', scatter_dimension=0, tiled=True)]
    pallas_call x0 -> x1, Pallas kernels: none -> 138 us  [layer_pass(): pl.pallas_call(functools.partial(layer_kernel, size), out_shape=[jax.Shap...]
    all_gather x2 -> x0, waiting for transfers between devices: 87 us -> none  [the longest x1 73 us: on_device(): image_full = lax.all_gather(images, 'chan', axis=0, tiled=True)]
    conv_general_dilated x5 -> x0, matrix products: 65.9 us -> none  [the longest x3 41.5 us: convolve(): lax.conv_general_dilated(left_view, kernel, (1, 1), ((1, 1), (1, 1)), dim...]
    unnamed x8 -> x6, waiting for transfers between devices: 0.79 us -> 57.7 us
    all_gather x2 -> x5, blocking collectives: 20.2 us -> 70 us  [the longest x1 18.1 us: on_device(): teacher_full = lax.all_gather(teacher_weight, 'chan', axis=1, tiled=True)]
    conv_general_dilated x2 -> x0, local copies, waits for them, and re-layouts: 38.2 us -> none  [convolve(): lax.conv_general_dilated(left_view, kernel, (1, 1), ((1, 1), (1, 1)), dim...]
    unnamed x2 -> x0, matrix products: 35.7 us -> none
  transfers between devices with their start and end apart: 6 -> 4, of which waited for: 4 -> 4; matrix products, arithmetic and copies ran while one was open for 27% -> 2% of each run, Pallas kernels for 0% -> 0%
where the time goes in v1:
time: 400 us; the launch traced here: 399 us
  Pallas kernels  138 us (34%)
  blocking collectives  109 us (27%)
  waiting for transfers between devices  108 us (27%)
  between operations  16.6 us (4%)
  local copies, waits for them, and re-layouts  16.4 us (4%)
  other arithmetic  11.2 us (3%)
    pallas_call x1, Pallas kernels, layer_pass(): pl.pallas_call(functools.partial(layer_kernel, size), out_shape=[jax.Shap...  138 us
    unnamed x6, waiting for transfers between devices  57.7 us
    psum x1, blocking collectives, on_device(): lax.psum(jnp.stack([jnp.sum(student_master * student_master), jnp.sum(upd...  38.5 us
    reduce_scatter x1, waiting for transfers between devices, on_device(): lax.psum_scatter(regress_part, 'dp', scatter_dimension=0, tiled=True)  31 us
    reduce_scatter x1, waiting for transfers between devices, on_device(): lax.psum_scatter(student_grad, 'chan', scatter_dimension=1, tiled=True)  19.1 us
    all_gather x1, blocking collectives, on_device(): teacher_full = lax.all_gather(teacher_weight, 'chan', axis=1, tiled=True)  18.1 us
    all_gather x1, blocking collectives, on_device(): student_full = lax.all_gather(student_full, 'chan', axis=1, tiled=True)  16.4 us
    all_gather x1, blocking collectives, on_device(): regress_full = lax.all_gather(regress_full, 'chan', axis=1, tiled=True)  15.4 us
  transfers between devices with their start and end apart: 4, of which 4 were waited for; matrix products, arithmetic and copies ran while one was open for 2% of the time, Pallas kernels for 0%

profile of v1, /device:TPU:0, one launch (start us, length us, event | category | flops | bytes accessed | tf_op | source)
XLA Modules:
  0.0 398.8 jit_solution(1887673529345060921)
XLA Ops:
  7.2 0.0 reduce-scatter.11.cloned.1.call-start
  7.2 0.8 convert_bitcast_fusion.1
  8.0 0.8 convert_bitcast_fusion
  8.9 10.7 %all-gather.1 = bf16[8,144,48]{1,2,0:T(8,128)(2,1)S(1)} all-gather(bf16[1,144,48]{1,2,0:T(8,128)(2,1)S(1)} %convert_bitcast_fusion.1), channel_id=1, replica_groups=mesh['dp'=8,'chan'=4] {'dp'}, dimensions={0}, use_global_device_ids=true | all-gather | bytes 124416 | tf_op jit(solution)/shard_map/all_gather | solution.py:445
  19.6 0.1 copy.94
  19.6 0.2 reshape.99
  19.9 9.3 %all-gather = bf16[8,144,64]{1,2,0:T(8,128)(2,1)S(1)} all-gather(bf16[1,144,64]{1,2,0:T(8,128)(2,1)S(1)} %convert_bitcast_fusion), channel_id=1, replica_groups=mesh['dp'=8,'chan'=4] {'dp'}, dimensions={0}, use_global_device_ids=true | all-gather | bytes 165888 | tf_op jit(solution)/shard_map/all_gather | solution.py:443
  29.2 0.1 copy.91
  29.3 0.3 reshape.97
  29.6 15.4 %all_gather.19 = bf16[1152,192]{0,1:T(8,128)(2,1)S(1)} all-gather(bf16[1152,48]{0,1:T(8,128)(2,1)S(1)} %reshape.99), channel_id=1, replica_groups=mesh['dp'=8,'chan'=4] {'chan'}, dimensions={1}, use_global_device_ids=true | all-gather | bytes 552960 | tf_op jit(solution)/shard_map/all_gather | solution.py:446
  45.0 16.4 %all_gather.16 = bf16[1152,256]{0,1:T(8,128)(2,1)S(1)} all-gather(bf16[1152,64]{0,1:T(8,128)(2,1)S(1)} %reshape.97), channel_id=1, replica_groups=mesh['dp'=8,'chan'=4] {'chan'}, dimensions={1}, use_global_device_ids=true | all-gather | bytes 737280 | tf_op jit(solution)/shard_map/all_gather | solution.py:444
  61.4 0.2 reshape.85
  61.7 0.1 copy.92
  61.7 0.2 copy.97
  62.0 0.3 copy.98
  62.3 1.1 copy.100.w_in_back
  63.4 0.0 copy-done
  63.4 0.2 copy.95
  63.7 0.0 copy-start.9
  63.7 0.3 copy.96
  64.0 1.0 copy.99.w_reg_back
  65.0 18.1 %all_gather.17 = bf16[1152,384]{0,1:T(8,128)(2,1)S(1)} all-gather(bf16[1152,96]{0,1:T(8,128)(2,1)S(1)} %copy-done.9), channel_id=1, replica_groups=mesh['dp'=8,'chan'=4] {'chan'}, dimensions={1}, use_global_device_ids=true | all-gather | bytes 1105920 | tf_op jit(solution)/shard_map/all_gather | solution.py:447
  83.2 0.3 reshape.87
  83.5 0.1 copy.93
  83.6 1.2 pad_maximum_fusion.w_in
  84.8 138.0 %layer.1 = (bf16[16,32,256]{2,1,0:T(8,128)(2,1)}, bf16[16,32,1024]{2,1,0:T(8,128)(2,1)}, f32[1152,256]{1,0:T(8,128)}, f32[1152,192]{1,0:T(8,128)}) custom-call(bf16[512,1024]{1,0:T(8,128)(2,1)} %bitcast.68, s32[512,1024]{1,0:T(8,128)} %bitcast.67, s32[768,1024]{1,0:T(8,128)} %bitcast.66, s32[512,256]{1,0:T(8,128)} %bitcast.69, bf16[512,256]{1,0:T(8,128)(2,1)} %bitcast.70, ...), custom_call_target="tpu_custom_call" | custom-call | flops 16307453952 | bytes 16777216 | tf_op jit(solution)/shard_map/layer/pallas_call | solution.py:340
  222.9 0.0 reduce-scatter.11.cloned.1.call-update
  222.9 0.2 reduce-scatter.13.cloned.1.call-start
  223.1 1.0 copy-done.1
  224.1 0.6 reshape.93
  224.8 0.7 copy.101
  225.5 0.8 reshape.94
  226.3 1.4 copy.107
  227.7 0.0 copy-start.3
  227.7 0.0 copy-start.14
  227.8 0.0 copy-start.15
  227.8 0.0 reduce-scatter.13.cloned.1.call-update
  227.8 0.0 reduce-scatter.15.cloned.1.call-start
  227.9 31.0 %reduce-scatter.11.cloned.1.call-done = f32[144,192]{1,0:T(8,128)} async-done(((f32[1152,192]{1,0:T(8,128)}), f32[144,192]{1,0:T(8,128)}) %reduce-scatter.11.cloned.1.call-update) | async-done | bytes 110608 | tf_op jit(solution)/shard_map/reduce_scatter | solution.py:469
  258.8 1.7 copy.109
  260.5 0.0 reduce-scatter.15.cloned.1.call-update
  260.5 0.0 reduce-scatter.9.cloned.1.call-start
  260.6 38.6 %reduce-scatter.13.cloned.1.call-done = f32[144,256]{1,0:T(8,128)} async-done(((f32[1152,256]{1,0:T(8,128)}), f32[144,256]{1,0:T(8,128)}) %reduce-scatter.13.cloned.1.call-update) | async-done | bytes 147472
  299.2 1.7 copy.108
  300.9 0.0 reduce-scatter.9.cloned.1.call-update
  301.0 0.9 copy.105
  301.8 19.0 %reduce-scatter.15.cloned.1.call-done = f32[48,144]{1,0:T(8,128)} async-done(((f32[192,144]{1,0:T(8,128)}), f32[48,144]{1,0:T(8,128)}) %reduce-scatter.15.cloned.1.call-update) | async-done | bytes 27664
  320.8 0.0 copy-done.16
  320.8 1.5 multiply_reduce_fusion.3
  322.3 19.1 %reduce-scatter.9.cloned.1.call-done = f32[144,64]{0,1:T(8,128)} async-done(((f32[144,256]{0,1:T(8,128)}), f32[144,64]{0,1:T(8,128)}) %reduce-scatter.9.cloned.1.call-update) | async-done | bytes 36880 | tf_op jit(solution)/shard_map/reduce_scatter | solution.py:468
  341.4 0.0 copy-done.3
  341.4 1.5 multiply_reduce_fusion.1
  342.9 2.7 pad_maximum_fusion.1
  345.7 0.0 copy-done.2
  345.7 1.6 copy.106
  347.2 38.5 %psum.7 = f32[4]{0:T(128)S(1)} all-reduce(f32[4]{0:T(128)S(1)} %pad_maximum_fusion.1), channel_id=1, replica_groups=mesh['dp'=8,'chan'=4] {'dp','chan'}, use_global_device_ids=true, to_apply=%region_8.0 | all-reduce | flops 4 | bytes 32 | tf_op jit(solution)/shard_map/psum | solution.py:473
  385.7 0.7 reshape.95
  386.4 0.6 fusion.8
  389.7 0.6 fusion.3
  390.3 0.6 multiply_add_fusion.3
  391.0 0.7 fusion.4
  391.6 0.0 copy-done.11
  391.6 0.0 copy-done.13
  391.6 0.6 multiply_add_fusion
  (30 shorter events, 0.1 us)
Async XLA Ops:
  7.2 251.6 %reduce-scatter.11.cloned.1.call-start = ((), (), s32[]{:S(2)}) async-start(), calls=%async_computation.5 | async-start | bytes 1327104 | tf_op jit(solution)/shard_map/reduce_scatter | solution.py:469
  45.0 18.4 %copy-start = (bf16[1152,192]{0,1:T(8,128)(2,1)}, bf16[1152,192]{0,1:T(8,128)(2,1)S(1)}, u32[]{:S(2)}) copy-start(bf16[1152,192]{0,1:T(8,128)(2,1)S(1)} %all_gather.19) | copy-start | bytes 1327108
  63.7 1.4 copy-start.9
  222.9 1.3 copy-start.1
  222.9 76.3 %reduce-scatter.13.cloned.1.call-start = ((), (), s32[]{:S(2)}) async-start(), calls=%async_computation.6 | async-start | bytes 1327104
  227.7 73.2 %copy-start.5 = (bf16[16,32,256]{2,1,0:T(8,128)(2,1)S(1)}, bf16[16,32,256]{2,1,0:T(8,128)(2,1)}, u32[]{:S(2)}) copy-start(bf16[16,32,256]{2,1,0:T(8,128)(2,1)} %get-tuple-element.17) | copy-start | bytes 786436
  227.7 93.1 %copy-start.4 = (f32[144,48]{0,1:T(8,128)S(1)}, f32[144,48]{0,1:T(8,128)}, u32[]{:S(2)}) copy-start(f32[144,48]{0,1:T(8,128)} %param.17) | copy-start | bytes 82948
  227.7 93.1 %copy-start.16 = (f32[144,48]{0,1:T(8,128)S(1)}, f32[144,48]{0,1:T(8,128)}, u32[]{:S(2)}) copy-start(f32[144,48]{0,1:T(8,128)} %param.27) | copy-start | bytes 82948
  227.7 93.1 %copy-start.17 = (f32[144,48]{0,1:T(8,128)S(1)}, f32[144,48]{0,1:T(8,128)}, u32[]{:S(2)}) copy-start(f32[144,48]{0,1:T(8,128)} %param.28) | copy-start | bytes 82948
  227.7 113.7 %copy-start.3 = (f32[144,64]{0,1:T(8,128)S(1)}, f32[144,64]{0,1:T(8,128)}, u32[]{:S(2)}) copy-start(f32[144,64]{0,1:T(8,128)} %param.16) | copy-start | bytes 110596
  227.7 113.7 %copy-start.14 = (f32[144,64]{0,1:T(8,128)S(1)}, f32[144,64]{0,1:T(8,128)}, u32[]{:S(2)}) copy-start(f32[144,64]{0,1:T(8,128)} %param.24) | copy-start | bytes 110596
  227.8 113.7 %copy-start.15 = (f32[144,64]{0,1:T(8,128)S(1)}, f32[144,64]{0,1:T(8,128)}, u32[]{:S(2)}) copy-start(f32[144,64]{0,1:T(8,128)} %param.25) | copy-start | bytes 110596
  227.8 117.9 %copy-start.2 = (bf16[16,32,1024]{2,1,0:T(8,128)(2,1)S(1)}, bf16[16,32,1024]{2,1,0:T(8,128)(2,1)}, u32[]{:S(2)}) copy-start(bf16[16,32,1024]{2,1,0:T(8,128)(2,1)} %get-tuple-element.18) | copy-start | bytes 3145732
  227.8 93.0 %reduce-scatter.15.cloned.1.call-start = ((), (), s32[]{:S(2)}) async-start(), calls=%async_computation.7 | async-start | bytes 245760
  260.5 80.9 %reduce-scatter.9.cloned.1.call-start = ((), (), s32[]{:S(2)}) async-start(), calls=%async_computation.4 | async-start | bytes 327680 | tf_op jit(solution)/shard_map/reduce_scatter | solution.py:468
  301.8 88.5 %copy-start.18 = (f32[144,48]{0,1:T(8,128)S(1)}, f32[144,48]{0,1:T(8,128)}, u32[]{:S(2)}) copy-start(f32[144,48]{0,1:T(8,128)} %param.29) | copy-start | bytes 82948
  322.3 69.3 %copy-start.10 = (f32[144,48]{0,1:T(8,128)}, f32[144,48]{0,1:T(8,128)S(1)}, u32[]{:S(2)}) copy-start(f32[144,48]{0,1:T(8,128)S(1)} %get-tuple-element.83) | copy-start | bytes 82948
  322.3 69.3 %copy-start.11 = (f32[144,48]{0,1:T(8,128)}, f32[144,48]{0,1:T(8,128)S(1)}, u32[]{:S(2)}) copy-start(f32[144,48]{0,1:T(8,128)S(1)} %get-tuple-element.84) | copy-start | bytes 82948
  342.9 49.3 %copy-start.7 = (f32[144,64]{0,1:T(8,128)}, f32[144,64]{0,1:T(8,128)S(1)}, u32[]{:S(2)}) copy-start(f32[144,64]{0,1:T(8,128)S(1)} %get-tuple-element.81) | copy-start | bytes 110596
  342.9 49.3 %copy-start.8 = (f32[144,64]{0,1:T(8,128)}, f32[144,64]{0,1:T(8,128)S(1)}, u32[]{:S(2)}) copy-start(f32[144,64]{0,1:T(8,128)S(1)} %get-tuple-element.82) | copy-start | bytes 110596
  342.9 48.7 %copy-start.13 = (f32[144,64]{0,1:T(8,128)S(1)}, f32[144,64]{0,1:T(8,128)}, u32[]{:S(2)}) copy-start(f32[144,64]{0,1:T(8,128)} %param.26) | copy-start | bytes 110596
  390.3 2.0 copy-start.12
  391.6 0.7 copy-start.6
Sparse Core Ops, SparseCore 0:
  223.0 35.7 reduce-scatter.10
  262.4 36.7 reduce-scatter.12
  301.4 19.3 reduce-scatter.14
  323.6 17.7 reduce-scatter.8

commit v2 on v1

v2 whole, which is shorter than its diff:
```python
import functools
import types

import jax
import jax.numpy as jnp
from jax import lax
from jax.experimental import pallas as pl
from jax.experimental.pallas import tpu as pltpu
from jax.sharding import PartitionSpec as P

IMG = 32
STEP = 10
HINT_WEIGHT = 0.1
LEARN_RATE = 0.5
BETA_ONE = 0.9
BETA_TWO = 0.999
EPSILON = 1e-06
DECAY = 0.01
EMA_KEEP = 0.75

MESH = pl.DeviceIdType.MESH
F32 = jnp.float32
BF16 = jnp.bfloat16
CHUNK = 256
LANES = 128


def dot(left, right):
    return jnp.dot(left, right, preferred_element_type=F32)


def dot_nt(left, right, precision=None):
    return lax.dot_general(
        left, right, (((1,), (1,)), ((), ())), precision=precision, preferred_element_type=F32
    )


def one_hot(shape, target, axis):
    at = lax.broadcasted_iota(jnp.int32, shape, axis)
    return jnp.where(at == target, 1.0, 0.0).astype(BF16)


def layer_kernel(size, names, *refs):
    r = types.SimpleNamespace(**dict(zip(names, refs)))
    n, batch, cl, tl, rl = size["n"], size["batch"], size["cl"], size["tl"], size["rl"]
    fused, group = size["fused"], size["group"]
    slots = batch // n
    chans, touts, regs = n * cl, n * tl, n * rl
    pixels = IMG * IMG
    cells = pixels // 4
    me = lax.axis_index("chan")
    row = lax.axis_index("dp")
    core, chip, pairs = row % 2, row // 2, group // 2
    held, send = r.held, r.send

    def beside(step):
        return lax.rem(me + step, n)

    def at_chan(index):
        return {"chan": index}

    def at_row(index):
        return {"dp": index}

    def remote(src, dst, out_sem, in_sem, device):
        return pltpu.make_async_remote_copy(
            src, dst, out_sem, in_sem, device_id=device, device_id_type=MESH
        )

    greeted = [at_chan(beside(step)) for step in range(1, n)]
    if fused:
        greeted += [at_row(lax.rem(row + step, group)) for step in range(1, group)]

    loads = [
        pltpu.make_async_copy(r.images, r.raw, r.load_sem.at[0]),
        pltpu.make_async_copy(r.cot, r.raw_cot, r.load_sem.at[1]),
    ]
    for src, dst in ((r.swin, r.swin_wide), (r.twin, r.twin_wide), (r.pwin, r.pwin_wide)):
        for j in range(dst.shape[0]):
            loads.append(
                pltpu.make_async_copy(
                    src.at[:, pl.ds(j * LANES, LANES)], dst.at[j], r.load_sem.at[len(loads)]
                )
            )
    for copy in loads:
        copy.start()

    barrier = pltpu.get_barrier_semaphore()
    for device in greeted:
        pl.semaphore_signal(barrier, inc=1, device_id=device, device_id_type=MESH)

    if fused:
        depth = r.student_master.shape[0]

        def block(index):
            return pl.ds(pl.multiple_of(index * depth, 16), depth)

        mine = block(row)
        r.filters[me, mine, :] = jnp.zeros((depth, r.filters.shape[2]), BF16)
        r.filters[me, mine, 0 : 2 * cl] = r.student_master[...].astype(BF16)
        r.filters[me, mine, 2 * cl : 2 * cl + rl] = r.regress_master[...].astype(BF16)
        r.filters[me, mine, LANES : LANES + 2 * tl] = r.teacher[mine, :]

    pl.semaphore_wait(barrier, len(greeted))

    if fused:
        filter_z = [
            remote(
                r.filters.at[me, mine],
                r.filters.at[me, mine],
                r.fz_send.at[step],
                r.fz_recv.at[step],
                at_chan(beside(step)),
            )
            for step in range(1, n)
        ]
        for copy in filter_z:
            copy.start()

    for copy in loads:
        copy.wait()
    for j in range(r.wide.shape[0]):
        r.wide[j] = r.raw[:, j * LANES : (j + 1) * LANES].astype(F32)
    for j in range(r.cot_wide.shape[0]):
        r.cot_wide[j] = r.raw_cot[:, j * LANES : (j + 1) * LANES].astype(F32)

    def in_copies(slot, step):
        to = beside(step)
        return (
            remote(
                send.at[slot, to],
                held.at[slot, me],
                r.in_send.at[slot, step],
                r.in_recv.at[slot, step],
                at_chan(to),
            ),
            remote(
                r.send_pool.at[slot, to],
                r.held_pool.at[slot, me],
                r.pool_in_send.at[slot, step],
                r.pool_in_recv.at[slot, step],
                at_chan(to),
            ),
        )

    def own_copies(slot):
        return (
            pltpu.make_async_copy(send.at[slot, me], held.at[slot, me], r.own_sem.at[slot, 0]),
            pltpu.make_async_copy(
                r.send_pool.at[slot, me], r.held_pool.at[slot, me], r.own_sem.at[slot, 1]
            ),
        )

    def lanes_of(index):
        return pl.ds(pl.multiple_of(index * cl, cl), cl)

    def out_copies(slot, step):
        to = beside(step)
        return (
            remote(
                r.low_part.at[slot, lanes_of(to)],
                r.grad_out.at[me * slots + slot],
                r.out_send.at[slot, step],
                r.out_recv.at[slot, step],
                at_chan(to),
            ),
            remote(
                r.pool_part.at[slot, lanes_of(to)],
                r.pool_out.at[me * slots + slot],
                r.pool_out_send.at[slot, step],
                r.pool_out_recv.at[slot, step],
                at_chan(to),
            ),
        )

    def own_out(slot):
        here = me * slots + slot
        return (
            pltpu.make_async_copy(
                r.low_part.at[slot, lanes_of(me)], r.grad_out.at[here], r.own_out_sem.at[slot, 0]
            ),
            pltpu.make_async_copy(
                r.pool_part.at[slot, lanes_of(me)], r.pool_out.at[here], r.own_out_sem.at[slot, 1]
            ),
        )

    def prepare(slot, carry):
        for to in range(n):
            first_row = to * slots + slot
            for src, dst, first, rows in (
                (r.wide, send, 0, cl),
                (r.swin_wide, send, cl, cl),
                (r.twin_wide, send, 2 * cl, tl),
                (r.pwin_wide, r.send_pool, 0, cl),
                (r.cot_wide, r.send_pool, cl, cl),
            ):
                for j in range(src.shape[0]):
                    dst[slot, to, first : first + rows, j * LANES : (j + 1) * LANES] = (
                        src[j, pl.ds(first_row, rows, stride=batch), :].astype(F32).astype(BF16)
                    )
        for step in range(1, n):
            for copy in in_copies(slot, step):
                copy.start()
        for copy in own_copies(slot):
            copy.start()
        return carry

    lax.fori_loop(0, slots, prepare, 0)

    lane = lax.broadcasted_iota(jnp.int32, (16, pixels), 1)
    row_of, col_of = lane // IMG, lane % IMG
    for which, bad in enumerate((row_of == 0, row_of == IMG - 1, col_of == 0, col_of == IMG - 1)):
        r.edge[which] = jnp.where(bad, 0.0, 1.0).astype(BF16)
    spot = lax.broadcasted_iota(jnp.int32, (1, pixels), 1)
    home = (spot // (2 * IMG)) * (IMG // 2) + (spot % IMG) // 2
    r.up[...] = one_hot((cells, pixels), home, 0)
    r.sgrad[...] = jnp.zeros_like(r.sgrad)
    r.rgrad[...] = jnp.zeros_like(r.rgrad)

    if fused:
        picked = 2 * cl + rl + 2 * tl
        at = lax.broadcasted_iota(jnp.int32, (picked, 1), 0)
        teach = at - 2 * cl - rl
        lane_at = jnp.where(
            at < 2 * cl,
            2 * (at % cl) + at // cl,
            jnp.where(at < 2 * cl + rl, at, LANES + 2 * (teach % tl) + teach // tl),
        )
        r.gather_rows[...] = one_hot((picked, r.filters.shape[2]), lane_at, 1)
        for z in range(n):
            at = lax.broadcasted_iota(jnp.int32, (LANES, 1), 0)
            col_at = jnp.where(
                at < 2 * cl,
                (at % 2) * chans + z * cl + at // 2,
                jnp.where(at < 2 * cl + rl, 2 * chans + z * rl + at - 2 * cl, -1),
            )
            r.spread[z] = one_hot((LANES, r.spread.shape[2]), col_at, 1)

        for copy in filter_z:
            copy.wait_recv()

        def filter_chip(step):
            to = lax.rem(chip + step, pairs)
            return remote(
                r.filters.at[:, mine],
                r.filters.at[:, mine],
                r.fx_send.at[step],
                r.fx_recv.at[step],
                at_row(2 * to + core),
            )

        def filter_core(step):
            rows = block(2 * lax.rem(chip + pairs - step, pairs) + core)
            return remote(
                r.filters.at[:, rows],
                r.filters.at[:, rows],
                r.fc_send.at[step],
                r.fc_recv.at[step],
                at_row(row + 1 - 2 * core),
            )

        for step in range(1, pairs):
            filter_chip(step).start()
        filter_core(0).start()
        for step in range(1, pairs):
            filter_chip(step).wait_recv()
            filter_core(step).start()
        for step in range(pairs):
            filter_core(step).wait_recv()

        for z in range(n):
            rows_of = dot_nt(r.gather_rows[...], r.filters[z]).astype(BF16)
            first = 0
            for dst, start, many in (
                (r.w_in, z * cl, cl),
                (r.w_in, chans + z * cl, cl),
                (r.w_reg, z * rl, rl),
                (r.w_in, 2 * chans + z * tl, tl),
                (r.w_in, 2 * chans + touts + z * tl, tl),
            ):
                dst[start : start + many, :] = rows_of[first : first + many, :]
                first += many
        for tap in range(9):
            rows = slice((8 - tap) * chans, (9 - tap) * chans)
            total = dot(r.filters[0, rows, 0:LANES], r.spread[0])
            for z in range(1, n):
                total += dot(r.filters[z, rows, 0:LANES], r.spread[z])
            total = total.astype(BF16)
            r.w_in_back[:, tap * 2 * chans : (tap + 1) * 2 * chans] = total[:, 0 : 2 * chans]
            r.w_reg_back[:, tap * regs : (tap + 1) * regs] = total[:, 2 * chans : 2 * chans + regs]

    def columns(load, rows, dst):
        def group(g, carry):
            first = pl.multiple_of(g * 16, 16)
            base = load(first)
            for ky in range(3):
                if ky == 1:
                    moved = base
                else:
                    moved = pltpu.roll(base, (pixels - IMG * (ky - 1)) % pixels, 1)
                    moved = moved * r.edge[0 if ky == 0 else 1]
                for kx in range(3):
                    if kx == 1:
                        tap = moved
                    else:
                        tap = pltpu.roll(moved, (pixels - (kx - 1)) % pixels, 1)
                        tap = tap * r.edge[2 if kx == 0 else 3]
                    dst[pl.ds((3 * ky + kx) * rows + first, 16), :] = tap
            return carry

        lax.fori_loop(0, rows // 16, group, 0)

    def chunks(body):
        def one(c, carry):
            body(pl.ds(pl.multiple_of(c * CHUNK, CHUNK), CHUNK))
            return carry

        lax.fori_loop(0, pixels // CHUNK, one, 0)

    def corner_of(here):
        at = lax.broadcasted_iota(jnp.int32, (1, CHUNK), 1)
        return (2 * ((at // IMG) % 2) + at % 2).astype(F32)

    if fused:
        parts = ((r.rgrad, r.rc_send, r.rc_recv, r.rx_send, r.rx_recv),
                 (r.sgrad, r.sc_send, r.sc_recv, r.sx_send, r.sx_recv))

        def core_copy(which):
            return remote(
                parts[which][1],
                parts[which][2],
                r.core_send.at[which],
                r.core_recv.at[which],
                at_row(row + 1 - 2 * core),
            )

        def start_core(which):
            grads, out = parts[which][:2]
            for pair in range(pairs):
                out[pair] = grads[block(2 * pair + 1 - core), :].astype(BF16)
            core_copy(which).start()

        def chip_copy(which, step):
            return remote(
                parts[which][3].at[step],
                parts[which][4].at[step],
                r.chip_send.at[which, step],
                r.chip_recv.at[which, step],
                at_row(2 * lax.rem(chip + step, pairs) + core),
            )

        def chan_copy(step):
            return remote(
                r.zs_send.at[step],
                r.zs_recv.at[step],
                r.chan_send.at[step],
                r.chan_recv.at[step],
                at_chan(beside(step)),
            )

        def row_norm(step):
            return remote(
                r.part_rows.at[row],
                r.part_rows.at[row],
                r.rn_send.at[step],
                r.rn_recv.at[step],
                at_row(lax.rem(row + step, group)),
            )

        def chan_norm(step):
            return remote(
                r.part_chans.at[me],
                r.part_chans.at[me],
                r.cn_send.at[step],
                r.cn_recv.at[step],
                at_chan(beside(step)),
            )

    def image(slot, carry):
        for step in range(1, n):
            for copy in in_copies(slot, step):
                copy.wait_recv()
        for copy in own_copies(slot):
            copy.wait()

        def image_rows(first):
            return held[slot, first // cl, pl.ds(pl.multiple_of(first % cl, 16), 16), :]

        columns(image_rows, chans, r.x_cols)
        r.pool_part[slot] = jnp.zeros((chans, cells), BF16)

        def head(here):
            pre = dot(r.w_in[0 : 2 * chans, :], r.x_cols[:, here])
            pick = held[slot, :, cl : 2 * cl, here].reshape(chans, CHUNK).astype(F32)
            value = jnp.where(pick > 0.5, pre[chans:], pre[:chans]).astype(BF16)
            r.out_low[:, here] = value
            cell_win = r.held_pool[slot, :, 0:cl, :].reshape(chans, cells)
            cell_cot = r.held_pool[slot, :, cl : 2 * cl, :].reshape(chans, cells)
            chosen = dot(cell_win, r.up[:, here]) == corner_of(here)
            spread = dot(cell_cot, r.up[:, here])
            r.pool_back[:, here] = jnp.where(chosen, spread, 0.0).astype(BF16)
            kept = jnp.where(chosen, value.astype(F32), 0.0).astype(BF16)
            part = dot_nt(kept, r.up[:, here])
            r.pool_part[slot] = (r.pool_part[slot].astype(F32) + part).astype(BF16)

        chunks(head)
        columns(lambda first: r.out_low[pl.ds(first, 16), :], chans, r.o_cols)

        spot_mask = r.mask[pl.ds(me * slots + slot, 1), :].astype(F32)
        count = jnp.sum(spot_mask, axis=1, keepdims=True)
        scale = HINT_WEIGHT * (pixels / count)

        def hints(here):
            teach = dot(r.w_in[2 * chans :, :], r.x_cols[:, here])
            pick = held[slot, :, 2 * cl :, here].reshape(touts, CHUNK).astype(F32)
            target = jnp.where(pick > 0.5, teach[touts:], teach[:touts])
            guess = dot(r.w_reg[...], r.o_cols[:, here])
            weight = scale * r.mask[pl.ds(me * slots + slot, 1), here].astype(F32)
            r.hint[:, here] = (weight * (guess - target)).astype(BF16)

        chunks(hints)
        columns(lambda first: r.hint[pl.ds(first, 16), :], regs, r.h_cols)
        r.rgrad[...] += dot_nt(r.o_cols[...], r.hint[...])
        if fused:
            pl.when(slot == slots - 1)(lambda: start_core(0))

        def back(here):
            total = dot(r.w_reg_back[...], r.h_cols[:, here]) + r.pool_back[:, here].astype(F32)
            pick = held[slot, :, cl : 2 * cl, here].reshape(chans, CHUNK).astype(F32) > 0.5
            r.pre_grad[0:chans, here] = jnp.where(pick, 0.0, total).astype(BF16)
            r.pre_grad[chans:, here] = jnp.where(pick, total, 0.0).astype(BF16)

        chunks(back)
        columns(lambda first: r.pre_grad[pl.ds(first, 16), :], 2 * chans, r.p_cols)
        r.sgrad[...] += dot_nt(r.x_cols[...], r.pre_grad[...])
        if fused:
            pl.when(slot == slots - 1)(lambda: start_core(1))

        def image_back(here):
            r.low_part[slot, :, here] = dot(r.w_in_back[...], r.p_cols[:, here]).astype(BF16)

        chunks(image_back)
        for step in range(1, n):
            for copy in out_copies(slot, step):
                copy.start()
        for copy in own_out(slot):
            copy.start()
        return carry

    lax.fori_loop(0, slots, image, 0)

    if fused:
        r.whole_grad[...] = jnp.zeros_like(r.whole_grad)
        for which, cols in ((0, slice(2 * chans, 2 * chans + regs)), (1, slice(0, 2 * chans))):
            grads, _, came, out, _ = parts[which]
            core_copy(which).wait_recv()
            for step in range(1, pairs):
                to = lax.rem(chip + step, pairs)
                out[step] = (grads[block(2 * to + core), :] + came[to].astype(F32)).astype(BF16)
                chip_copy(which, step).start()
            r.whole_grad[:, cols] = grads[block(row), :] + came[chip].astype(F32)
        for which, cols in ((0, slice(2 * chans, 2 * chans + regs)), (1, slice(0, 2 * chans))):
            came = parts[which][4]
            for step in range(1, pairs):
                chip_copy(which, step).wait_recv()
            total = r.whole_grad[:, cols]
            for step in range(1, pairs):
                total += came[step].astype(F32)
            r.whole_grad[:, cols] = total
        low_grad = r.whole_grad[...].astype(BF16)
        for step in range(1, n):
            r.zs_send[step] = dot_nt(low_grad, r.spread[beside(step)]).astype(BF16)
            chan_copy(step).start()
        total = dot_nt(
            r.whole_grad[...], r.spread[me].astype(F32), precision=lax.Precision.HIGHEST
        )
        for step in range(1, n):
            chan_copy(step).wait_recv()
        for step in range(1, n):
            total += r.zs_recv[step].astype(F32)
        r.grad_sum[...] = total
        shifted = pltpu.roll(total, LANES - 2 * cl, 1)
        student, regress = r.student_master[...], r.regress_master[...]
        upd_s = lamb_update(student, total[:, 0 : 2 * cl], r.mom_student[...], r.sq_student[...])[2]
        upd_r = lamb_update(regress, shifted[:, 0:rl], r.mom_regress[...], r.sq_regress[...])[2]
        place = lax.broadcasted_iota(jnp.int32, (8, LANES), 1)
        tile = jnp.zeros((8, LANES), F32)
        for index, value in enumerate((student, upd_s, regress, upd_r)):
            square = jnp.sum(jnp.sum(value * value, axis=1, keepdims=True), axis=0, keepdims=True)
            tile = jnp.where(place == index, square, tile)
        r.part_rows[row] = tile
        for step in range(1, group):
            row_norm(step).start()
        for step in range(1, group):
            row_norm(step).wait_recv()
        tile = r.part_rows[0]
        for index in range(1, group):
            tile += r.part_rows[index]
        r.part_chans[me] = tile
        for step in range(1, n):
            chan_norm(step).start()
        for step in range(1, n):
            chan_norm(step).wait_recv()
        tile = r.part_chans[0]
        for index in range(1, n):
            tile += r.part_chans[index]
        r.sums[...] = tile

    def finish(slot, carry):
        for step in range(1, n):
            for copy in in_copies(slot, step):
                copy.wait_send()
            for copy in out_copies(slot, step):
                copy.wait()
        for copy in own_out(slot):
            copy.wait()
        return carry

    lax.fori_loop(0, slots, finish, 0)
    if fused:
        for step in range(1, n):
            filter_z[step - 1].wait_send()
            chan_copy(step).wait_send()
            chan_norm(step).wait_send()
        for step in range(1, group):
            row_norm(step).wait_send()
        for step in range(pairs):
            filter_core(step).wait_send()
        for step in range(1, pairs):
            filter_chip(step).wait_send()
        for which in range(2):
            core_copy(which).wait_send()
            for step in range(1, pairs):
                chip_copy(which, step).wait_send()


def lamb_update(weights, grads, moment, second):
    moment_new = BETA_ONE * moment + (1.0 - BETA_ONE) * grads
    second_new = BETA_TWO * second + (1.0 - BETA_TWO) * grads * grads
    moment_hat = moment_new / (1.0 - BETA_ONE**STEP)
    second_hat = second_new / (1.0 - BETA_TWO**STEP)
    update = moment_hat / (jnp.sqrt(second_hat) + EPSILON) + DECAY * weights
    return (moment_new, second_new, update)


def layer_pass(n, group, fused, arrays):
    cl, batch, pixels = arrays["images"].shape
    tl = arrays["twin"].shape[0]
    cells = arrays["pwin"].shape[2]
    slots = batch // n
    chans = n * cl
    if fused:
        rl = arrays["regress_master"].shape[1]
        depth = arrays["student_master"].shape[0]
    else:
        rl = arrays["w_reg"].shape[0] // n
    regs, touts, pairs = n * rl, n * tl, group // 2
    size = dict(n=n, batch=batch, cl=cl, tl=tl, rl=rl, fused=fused, group=group)
    vmem = pl.BlockSpec(memory_space=pltpu.VMEM)
    in_hbm = ("images", "swin", "twin", "pwin", "cot")
    ins = {
        name: a.reshape(a.shape[0] * a.shape[1], a.shape[2]) if name in in_hbm else a
        for name, a in arrays.items()
    }
    outs = {
        "pool_out": jax.ShapeDtypeStruct((batch, cl, cells), BF16),
        "grad_out": jax.ShapeDtypeStruct((batch, cl, pixels), BF16),
    }
    grads = {"sgrad": (9 * chans, 2 * chans), "rgrad": (9 * chans, regs)}
    dma = lambda *shape: pltpu.SemaphoreType.DMA(shape)
    scratch = {
        "raw": pltpu.VMEM((cl * batch, pixels), BF16),
        "raw_cot": pltpu.VMEM((cl * batch, cells), BF16),
        "wide": pltpu.VMEM((pixels // LANES, cl * batch, LANES), F32),
        "swin_wide": pltpu.VMEM((pixels // LANES, cl * batch, LANES), jnp.int32),
        "twin_wide": pltpu.VMEM((pixels // LANES, tl * batch, LANES), jnp.int32),
        "pwin_wide": pltpu.VMEM((cells // LANES, cl * batch, LANES), jnp.int32),
        "cot_wide": pltpu.VMEM((cells // LANES, cl * batch, LANES), F32),
        "load_sem": dma(2 + 2 * (pixels // LANES) + cells // LANES),
        "send": pltpu.VMEM((slots, n, 2 * cl + tl, pixels), BF16),
        "send_pool": pltpu.VMEM((slots, n, 2 * cl, cells), BF16),
        "held": pltpu.VMEM((slots, n, 2 * cl + tl, pixels), BF16),
        "held_pool": pltpu.VMEM((slots, n, 2 * cl, cells), BF16),
        "low_part": pltpu.VMEM((slots, chans, pixels), BF16),
        "pool_part": pltpu.VMEM((slots, chans, cells), BF16),
        "edge": pltpu.VMEM((4, 16, pixels), BF16),
        "up": pltpu.VMEM((cells, pixels), BF16),
        "x_cols": pltpu.VMEM((9 * chans, pixels), BF16),
        "o_cols": pltpu.VMEM((9 * chans, pixels), BF16),
        "h_cols": pltpu.VMEM((9 * regs, pixels), BF16),
        "p_cols": pltpu.VMEM((9 * 2 * chans, pixels), BF16),
        "out_low": pltpu.VMEM((chans, pixels), BF16),
        "pool_back": pltpu.VMEM((chans, pixels), BF16),
        "hint": pltpu.VMEM((regs, pixels), BF16),
        "pre_grad": pltpu.VMEM((2 * chans, pixels), BF16),
        "own_sem": dma(slots, 2),
        "own_out_sem": dma(slots, 2),
    }
    for name in ("in", "pool_in", "out", "pool_out"):
        scratch[name + "_send"] = dma(slots, n)
        scratch[name + "_recv"] = dma(slots, n)
    if fused:
        cols = 2 * chans + 2 * LANES
        outs["grad_sum"] = jax.ShapeDtypeStruct((depth, LANES), F32)
        outs["sums"] = jax.ShapeDtypeStruct((8, LANES), F32)
        scratch.update({name: pltpu.VMEM(shape, F32) for name, shape in grads.items()})
        scratch.update(
            {
                "filters": pltpu.VMEM((n, 9 * chans, 2 * LANES), BF16),
                "gather_rows": pltpu.VMEM((2 * cl + rl + 2 * tl, 2 * LANES), BF16),
                "spread": pltpu.VMEM((n, LANES, cols), BF16),
                "w_in": pltpu.VMEM((2 * chans + 2 * touts, 9 * chans), BF16),
                "w_reg": pltpu.VMEM((regs, 9 * chans), BF16),
                "w_reg_back": pltpu.VMEM((chans, 9 * regs), BF16),
                "w_in_back": pltpu.VMEM((chans, 9 * 2 * chans), BF16),
                "rc_send": pltpu.VMEM((pairs, depth, regs), BF16),
                "rc_recv": pltpu.VMEM((pairs, depth, regs), BF16),
                "rx_send": pltpu.VMEM((pairs, depth, regs), BF16),
                "rx_recv": pltpu.VMEM((pairs, depth, regs), BF16),
                "sc_send": pltpu.VMEM((pairs, depth, 2 * chans), BF16),
                "sc_recv": pltpu.VMEM((pairs, depth, 2 * chans), BF16),
                "sx_send": pltpu.VMEM((pairs, depth, 2 * chans), BF16),
                "sx_recv": pltpu.VMEM((pairs, depth, 2 * chans), BF16),
                "whole_grad": pltpu.VMEM((depth, cols), F32),
                "zs_send": pltpu.VMEM((n, depth, LANES), BF16),
                "zs_recv": pltpu.VMEM((n, depth, LANES), BF16),
                "part_rows": pltpu.VMEM((group, 8, LANES), F32),
                "part_chans": pltpu.VMEM((n, 8, LANES), F32),
                "core_send": dma(2),
                "core_recv": dma(2),
                "chip_send": dma(2, pairs),
                "chip_recv": dma(2, pairs),
            }
        )
        for name, many in (
            ("fz", n), ("fx", pairs), ("fc", pairs), ("chan", n), ("rn", group), ("cn", n)
        ):
            scratch[name + "_send"] = dma(many)
            scratch[name + "_recv"] = dma(many)
    else:
        outs.update({name: jax.ShapeDtypeStruct(shape, F32) for name, shape in grads.items()})
    flops = 2 * slots * pixels * 9 * chans * (3 * 2 * chans + 2 * touts + 3 * regs)
    names = tuple(ins) + tuple(outs) + tuple(scratch)
    return pl.pallas_call(
        functools.partial(layer_kernel, size, names),
        out_shape=list(outs.values()),
        in_specs=[
            pl.BlockSpec(memory_space=pl.ANY) if name in in_hbm else vmem for name in ins
        ],
        out_specs=[vmem] * len(outs),
        scratch_shapes=list(scratch.values()),
        compiler_params=pltpu.CompilerParams(
            collective_id=0, has_side_effects=True, vmem_limit_bytes=58 << 20
        ),
        cost_estimate=pl.CostEstimate(flops=flops, bytes_accessed=16 << 20, transcendentals=0),
        name="layer",
    )(*ins.values())


def split_pieces(weights):
    rows, cols = weights.shape
    return weights.reshape(rows, cols // 2, 2).transpose(2, 1, 0).reshape(cols, rows)


def back_weights(weights, outs):
    channels = weights.shape[0] // 9
    taps = weights.reshape(9, channels, outs)[::-1]
    return taps.transpose(1, 0, 2).reshape(channels, 9 * outs)


def gathered_filters(student_master, regress_master, teacher_weight):
    student_full = lax.all_gather(student_master.astype(BF16), "dp", axis=0, tiled=True)
    student_full = lax.all_gather(student_full, "chan", axis=1, tiled=True)
    regress_full = lax.all_gather(regress_master.astype(BF16), "dp", axis=0, tiled=True)
    regress_full = lax.all_gather(regress_full, "chan", axis=1, tiled=True)
    teacher_full = lax.all_gather(teacher_weight, "chan", axis=1, tiled=True)
    student_rows = split_pieces(student_full)
    return {
        "w_in": jnp.concatenate([student_rows, split_pieces(teacher_full)], axis=0),
        "w_reg": regress_full.T,
        "w_reg_back": back_weights(regress_full, regress_full.shape[1]),
        "w_in_back": back_weights(student_rows.T, student_full.shape[1]),
    }


def scattered_grads(student_part, regress_part):
    souts = student_part.shape[1]
    student_part = student_part.reshape(-1, 2, souts // 2).transpose(0, 2, 1).reshape(-1, souts)
    student_grad = lax.psum_scatter(student_part, "dp", scatter_dimension=0, tiled=True)
    student_grad = lax.psum_scatter(student_grad, "chan", scatter_dimension=1, tiled=True)
    regress_grad = lax.psum_scatter(regress_part, "dp", scatter_dimension=0, tiled=True)
    regress_grad = lax.psum_scatter(regress_grad, "chan", scatter_dimension=1, tiled=True)
    return student_grad, regress_grad


def on_device(
    n,
    group,
    images,
    student_master,
    regress_master,
    teacher_weight,
    student_win,
    teacher_win,
    pool_win,
    hint_mask,
    cotangent,
    mom_student,
    sq_student,
    ema_student,
    mom_regress,
    sq_regress,
    ema_regress,
):
    depth = student_master.shape[0]
    fused = group % 2 == 0 and depth % 16 == 0
    arrays = dict(
        images=images,
        swin=student_win,
        twin=teacher_win,
        pwin=pool_win,
        cot=cotangent,
        mask=hint_mask,
    )
    if fused:
        arrays.update(
            student_master=student_master,
            regress_master=regress_master,
            teacher=teacher_weight,
            mom_student=mom_student,
            sq_student=sq_student,
            mom_regress=mom_regress,
            sq_regress=sq_regress,
        )
        pooled, image_grad, grad_sum, sums = layer_pass(n, group, fused, arrays)
        souts, regs = student_master.shape[1], regress_master.shape[1]
        student_grad = grad_sum[:, 0:souts]
        regress_grad = grad_sum[:, souts : souts + regs]
    else:
        arrays.update(gathered_filters(student_master, regress_master, teacher_weight))
        pooled, image_grad, student_part, regress_part = layer_pass(n, group, fused, arrays)
        student_grad, regress_grad = scattered_grads(student_part, regress_part)
    mom_s, sq_s, upd_s = lamb_update(student_master, student_grad, mom_student, sq_student)
    mom_r, sq_r, upd_r = lamb_update(regress_master, regress_grad, mom_regress, sq_regress)
    if fused:
        all_sums = sums[0, 0:4]
    else:
        all_sums = lax.psum(
            jnp.stack(
                [jnp.sum(v * v) for v in (student_master, upd_s, regress_master, upd_r)]
            ),
            ("dp", "chan"),
        )
    norms = jnp.sqrt(all_sums)
    new_student = student_master - LEARN_RATE * (norms[0] / norms[1]) * upd_s
    new_regress = regress_master - LEARN_RATE * (norms[2] / norms[3]) * upd_r
    ema_s = EMA_KEEP * ema_student + (1.0 - EMA_KEEP) * new_student
    ema_r = EMA_KEEP * ema_regress + (1.0 - EMA_KEEP) * new_regress
    return (
        pooled.transpose(1, 0, 2),
        image_grad.transpose(1, 0, 2),
        new_student,
        mom_s,
        sq_s,
        ema_s,
        new_student.astype(BF16),
        new_regress,
        mom_r,
        sq_r,
        ema_r,
        new_regress.astype(BF16),
        norms.reshape(2, 2),
    )


def solution(mesh):
    acts = P("chan", "dp", None)
    rows = P("dp", "chan")
    in_specs = (
        (acts, rows, rows, P(None, "chan"))
        + (acts, acts, acts, P("dp", None), acts)
        + (rows,) * 6
    )
    out_specs = (acts, acts) + (rows,) * 10 + (P(),)
    return jax.shard_map(
        functools.partial(on_device, mesh.shape["chan"], mesh.shape["dp"]),
        mesh=mesh,
        in_specs=in_specs,
        out_specs=out_specs,
        check_vma=False,
    )
```

time: 400 us -> 189 us (0.47)
  blocking collectives: 109 us -> 0 us
  waiting for transfers between devices: 108 us -> 0 us
  Pallas kernels: 138 us -> 160 us
  between operations: 16.6 us -> 3.48 us
  other arithmetic: 11.2 us -> 2.01 us
  local copies, waits for them, and re-layouts: 16.4 us -> 22.8 us
    all_gather x5 -> x0, blocking collectives: 70 us -> none  [the longest x1 18.1 us: on_device(): teacher_full = lax.all_gather(teacher_weight, 'chan', axis=1, tiled=True)]
    unnamed x6 -> x0, waiting for transfers between devices: 57.7 us -> none
    reduce_scatter x2 -> x0, waiting for transfers between devices: 50 us -> none  [the longest x1 31 us: on_device(): lax.psum_scatter(regress_part, 'dp', scatter_dimension=0, tiled=True)]
    psum x1 -> x0, blocking collectives: 38.5 us -> none  [on_device(): lax.psum(jnp.stack([jnp.sum(student_master * student_master), jnp.sum(upd...]
    pallas_call x1, Pallas kernels: 138 us -> 160 us  [layer_pass(): pl.pallas_call(functools.partial(layer_kernel, size, names), out_shape=li...]
    unnamed x45 -> x41, local copies, waits for them, and re-layouts: 8.81 us -> 20.8 us
    reshape x8 -> x0, local copies, waits for them, and re-layouts: 4.8 us -> none  [the longest x2 2.08 us: back_weights(): return taps.transpose(1, 0, 2).reshape(channels, 9 * outs)]
  transfers between devices with their start and end apart: 4 -> 0, of which waited for: 4 -> 0; matrix products, arithmetic and copies ran while one was open for 2% -> 0% of each run, Pallas kernels for 0% -> 0%
where the time goes in v2:
time: 189 us; the launch traced here: 188 us
  Pallas kernels  160 us (85%)
  local copies, waits for them, and re-layouts  22.8 us (12%)
  between operations  3.48 us (2%)
  other arithmetic  2.01 us (1%)
    pallas_call x1, Pallas kernels, layer_pass(): pl.pallas_call(functools.partial(layer_kernel, size, names), out_shape=li...  160 us
    unnamed x41, local copies, waits for them, and re-layouts  20.8 us

profile of v2, /device:TPU:0, one launch (start us, length us, event | category | flops | bytes accessed | tf_op | source)
XLA Modules:
  0.0 188.1 jit_solution(11254482005983093927)
XLA Ops:
  0.6 1.6 copy.57.refs_6_
  2.2 1.5 copy.58.refs_7_
  3.7 1.6 copy.60.refs_9_
  5.3 1.6 copy.61.refs_10_
  6.9 1.5 copy.62.refs_11_
  8.4 1.5 copy.63.refs_12_
  9.9 1.8 copy.59.refs_8_
  11.7 0.0 copy-start.4
  11.7 0.0 copy-start.5
  11.7 0.0 copy-start.6
  11.7 0.0 copy-start.9
  11.7 0.0 copy-start.1
  11.8 0.0 copy-start.2
  11.8 0.0 copy-start.3
  11.8 0.0 copy-start.8
  11.8 159.8 %layer.1 = (bf16[16,32,256]{2,1,0:T(8,128)(2,1)}, bf16[16,32,1024]{2,1,0:T(8,128)(2,1)}, f32[144,128]{1,0:T(8,128)}, f32[8,128]{1,0:T(8,128)}) custom-call(bf16[512,1024]{1,0:T(8,128)(2,1)} %bitcast.13, s32[512,1024]{1,0:T(8,128)} %bitcast.12, s32[768,1024]{1,0:T(8,128)} %bitcast.11, s32[512,256]{1,0:T(8,128)} %bitcast.14, bf16[512,256]{1,0:T(8,128)(2,1)} %bitcast.15, ...), custom_call_target="tpu_custom_call" | custom-call | flops 16307453952 | bytes 16777216 | tf_op jit(solution)/shard_map/layer/pallas_call | solution.py:644
  171.6 0.0 copy-start
  171.6 0.0 copy-start.7
  171.6 0.8 fusion.2
  172.4 0.6 fusion.7
  174.3 0.0 copy-done.4
  174.4 0.0 copy-done.5
  174.4 0.0 copy-done.6
  174.4 1.0 fusion.3
  175.4 0.0 copy-done.9
  175.4 0.1 copy.75
  175.5 0.7 copy.86
  176.2 0.7 copy.83
  178.3 0.0 copy-done.1
  178.3 0.0 copy-done.2
  178.3 0.0 copy-done.3
  178.3 1.0 fusion.5
  179.3 0.0 copy-done.8
  179.3 0.1 copy.69
  179.4 0.7 copy.81
  180.1 0.7 copy.78
  180.8 0.7 copy.84
  181.5 0.7 copy.85
  182.2 0.7 copy.87
  182.9 0.7 copy.79
  183.6 0.7 copy.80
  184.3 0.7 copy.82
  185.0 0.6 sqrt.17
  185.7 0.0 copy-done
  185.7 1.5 copy.77
  187.2 0.0 copy-done.7
  187.2 0.9 copy.76
  (2 shorter events, 0.0 us)
Async XLA Ops:
  11.7 162.6 %copy-start.4 = (f32[144,48]{1,0:T(8,128)S(1)}, f32[144,48]{1,0:T(8,128)}, u32[]{:S(2)}) copy-start(f32[144,48]{1,0:T(8,128)} %copy.58.refs_7_) | copy-start | bytes 82948
  11.7 162.6 %copy-start.5 = (f32[144,48]{1,0:T(8,128)S(1)}, f32[144,48]{1,0:T(8,128)}, u32[]{:S(2)}) copy-start(f32[144,48]{1,0:T(8,128)} %copy.62.refs_11_) | copy-start | bytes 82948
  11.7 162.6 %copy-start.6 = (f32[144,48]{1,0:T(8,128)S(1)}, f32[144,48]{1,0:T(8,128)}, u32[]{:S(2)}) copy-start(f32[144,48]{1,0:T(8,128)} %copy.63.refs_12_) | copy-start | bytes 82948
  11.7 163.7 %copy-start.9 = (f32[144,48]{0,1:T(8,128)S(1)}, f32[144,48]{0,1:T(8,128)}, u32[]{:S(2)}) copy-start(f32[144,48]{0,1:T(8,128)} %param.29) | copy-start | bytes 82948
  11.7 166.5 %copy-start.1 = (f32[144,64]{1,0:T(8,128)S(1)}, f32[144,64]{1,0:T(8,128)}, u32[]{:S(2)}) copy-start(f32[144,64]{1,0:T(8,128)} %copy.57.refs_6_) | copy-start | bytes 110596
  11.8 166.5 %copy-start.2 = (f32[144,64]{1,0:T(8,128)S(1)}, f32[144,64]{1,0:T(8,128)}, u32[]{:S(2)}) copy-start(f32[144,64]{1,0:T(8,128)} %copy.60.refs_9_) | copy-start | bytes 110596
  11.8 166.5 %copy-start.3 = (f32[144,64]{1,0:T(8,128)S(1)}, f32[144,64]{1,0:T(8,128)}, u32[]{:S(2)}) copy-start(f32[144,64]{1,0:T(8,128)} %copy.61.refs_10_) | copy-start | bytes 110596
  11.8 167.5 %copy-start.8 = (f32[144,64]{0,1:T(8,128)S(1)}, f32[144,64]{0,1:T(8,128)}, u32[]{:S(2)}) copy-start(f32[144,64]{0,1:T(8,128)} %param.26) | copy-start | bytes 110596
  171.6 14.1 %copy-start = (bf16[16,32,1024]{2,1,0:T(8,128)(2,1)S(1)}, bf16[16,32,1024]{2,1,0:T(8,128)(2,1)}, u32[]{:S(2)}) copy-start(bf16[16,32,1024]{2,1,0:T(8,128)(2,1)} %get-tuple-element.18) | copy-start | bytes 3145732
  171.6 15.6 %copy-start.7 = (bf16[16,32,256]{2,1,0:T(8,128)(2,1)S(1)}, bf16[16,32,256]{2,1,0:T(8,128)(2,1)}, u32[]{:S(2)}) copy-start(bf16[16,32,256]{2,1,0:T(8,128)(2,1)} %get-tuple-element.17) | copy-start | bytes 786436

commit v3 on v2

--- a/solution.py
+++ b/solution.py
@@ -90,16 +90,20 @@
         pl.semaphore_signal(barrier, inc=1, device_id=device, device_id_type=MESH)
 
     if fused:
-        depth = r.student_master.shape[0]
+        depth = r.student_t.shape[1]
 
         def block(index):
             return pl.ds(pl.multiple_of(index * depth, 16), depth)
 
         mine = block(row)
-        r.filters[me, mine, :] = jnp.zeros((depth, r.filters.shape[2]), BF16)
-        r.filters[me, mine, 0 : 2 * cl] = r.student_master[...].astype(BF16)
-        r.filters[me, mine, 2 * cl : 2 * cl + rl] = r.regress_master[...].astype(BF16)
-        r.filters[me, mine, LANES : LANES + 2 * tl] = r.teacher[mine, :]
+        r.flat[...] = jnp.zeros_like(r.flat)
+        r.flat[0 : 2 * cl, 0:depth] = r.student_t[...]
+        r.flat[2 * cl : 2 * cl + rl, 0:depth] = r.regress_t[...]
+        r.filters[me, mine, 0:LANES] = r.flat[...].T[0:depth, :].astype(BF16)
+        r.teach_flat[...] = jnp.zeros_like(r.teach_flat)
+        r.teach_flat[0 : 2 * tl, :] = r.teacher_t[...].astype(F32)
+        r.teach_cols[...] = r.teach_flat[...].T
+        r.filters[me, mine, LANES:] = r.teach_cols[mine, :].astype(BF16)
 
     pl.semaphore_wait(barrier, len(greeted))
 
@@ -183,6 +187,15 @@
                 r.pool_part.at[slot, lanes_of(me)], r.pool_out.at[here], r.own_out_sem.at[slot, 1]
             ),
         )
+
+    def start_out(slot):
+        for step in range(1, n):
+            for copy in out_copies(slot, step):
+                copy.start()
+
+    def start_early():
+        for slot in range(slots - 1):
+            start_out(slot)
 
     def prepare(slot, carry):
         for to in range(n):
@@ -308,7 +321,7 @@
                     dst[pl.ds((3 * ky + kx) * rows + first, 16), :] = tap
             return carry
 
-        lax.fori_loop(0, rows // 16, group, 0)
+        lax.fori_loop(0, rows // 16, group, 0, unroll=2)
 
     def chunks(body):
         def one(c, carry):
@@ -382,6 +395,7 @@
                 copy.wait_recv()
         for copy in own_copies(slot):
             copy.wait()
+        pl.when(slot == slots - 1)(start_early)
 
         def image_rows(first):
             return held[slot, first // cl, pl.ds(pl.multiple_of(first % cl, 16), 16), :]
@@ -440,9 +454,7 @@
             r.low_part[slot, :, here] = dot(r.w_in_back[...], r.p_cols[:, here]).astype(BF16)
 
         chunks(image_back)
-        for step in range(1, n):
-            for copy in out_copies(slot, step):
-                copy.start()
+        pl.when(slot == slots - 1)(lambda: start_out(slots - 1))
         for copy in own_out(slot):
             copy.start()
         return carry
@@ -478,11 +490,14 @@
             chan_copy(step).wait_recv()
         for step in range(1, n):
             total += r.zs_recv[step].astype(F32)
+        r.tall[0:depth, :] = total
+        total = r.tall[...].T[:, 0:depth]
         r.grad_sum[...] = total
-        shifted = pltpu.roll(total, LANES - 2 * cl, 1)
-        student, regress = r.student_master[...], r.regress_master[...]
-        upd_s = lamb_update(student, total[:, 0 : 2 * cl], r.mom_student[...], r.sq_student[...])[2]
-        upd_r = lamb_update(regress, shifted[:, 0:rl], r.mom_regress[...], r.sq_regress[...])[2]
+        student, regress = r.student_t[...], r.regress_t[...]
+        upd_s = lamb_update(student, total[0 : 2 * cl], r.mom_student[...], r.sq_student[...])[2]
+        upd_r = lamb_update(
+            regress, total[2 * cl : 2 * cl + rl], r.mom_regress[...], r.sq_regress[...]
+        )[2]
         place = lax.broadcasted_iota(jnp.int32, (8, LANES), 1)
         tile = jnp.zeros((8, LANES), F32)
         for index, value in enumerate((student, upd_s, regress, upd_r)):
@@ -550,8 +565,7 @@
     slots = batch // n
     chans = n * cl
     if fused:
-        rl = arrays["regress_master"].shape[1]
-        depth = arrays["student_master"].shape[0]
+        rl, depth = arrays["regress_t"].shape
     else:
         rl = arrays["w_reg"].shape[0] // n
     regs, touts, pairs = n * rl, n * tl, group // 2
@@ -601,11 +615,16 @@
         scratch[name + "_recv"] = dma(slots, n)
     if fused:
         cols = 2 * chans + 2 * LANES
-        outs["grad_sum"] = jax.ShapeDtypeStruct((depth, LANES), F32)
+        tall = -(-depth // LANES) * LANES
+        outs["grad_sum"] = jax.ShapeDtypeStruct((LANES, depth), F32)
         outs["sums"] = jax.ShapeDtypeStruct((8, LANES), F32)
         scratch.update({name: pltpu.VMEM(shape, F32) for name, shape in grads.items()})
         scratch.update(
             {
+                "flat": pltpu.VMEM((LANES, tall), F32),
+                "tall": pltpu.VMEM((tall, LANES), F32),
+                "teach_flat": pltpu.VMEM((LANES, 9 * chans), F32),
+                "teach_cols": pltpu.VMEM((9 * chans, LANES), F32),
                 "filters": pltpu.VMEM((n, 9 * chans, 2 * LANES), BF16),
                 "gather_rows": pltpu.VMEM((2 * cl + rl + 2 * tl, 2 * LANES), BF16),
                 "spread": pltpu.VMEM((n, LANES, cols), BF16),
@@ -657,6 +676,75 @@
     )(*ins.values())
 
 
+def final_kernel(batch, *refs):
+    wide, came_sem = refs[-2:]
+    came = []
+    for index, (src, dst) in enumerate(zip(refs[0:4], refs[-6:-2])):
+        came.append(pltpu.make_async_copy(src, dst, came_sem.at[index]))
+        came[-1].start()
+    pool_in, grad_in, grad_sum, sums = refs[-6:-2]
+    student, regress, mom_s, sq_s, mom_r, sq_r, ema_s, ema_r = refs[4:12]
+    pooled, image_grad, new_s, new_r, trust = refs[12], refs[13], refs[14:19], refs[19:24], refs[24]
+    came[2].wait()
+    came[3].wait()
+    norm = [jnp.sqrt(sums[0:1, k : k + 1]) for k in range(4)]
+    souts, regs = student.shape[0], regress.shape[0]
+    for weights, grads, moment, second, average, outs, top, bottom in (
+        (student, grad_sum[0:souts, :], mom_s, sq_s, ema_s, new_s, norm[0], norm[1]),
+        (regress, grad_sum[souts : souts + regs, :], mom_r, sq_r, ema_r, new_r, norm[2], norm[3]),
+    ):
+        moment_new, second_new, update = lamb_update(
+            weights[...], grads, moment[...], second[...]
+        )
+        new = weights[...] - LEARN_RATE * (top / bottom) * update
+        outs[0][...] = new
+        outs[1][...] = moment_new
+        outs[2][...] = second_new
+        outs[3][...] = EMA_KEEP * average[...] + (1.0 - EMA_KEEP) * new
+        outs[4][...] = new.astype(BF16)
+    across = lax.broadcasted_iota(jnp.int32, (2, 2), 1)
+    down = lax.broadcasted_iota(jnp.int32, (2, 2), 0)
+    first = jnp.where(across == 0, norm[0], norm[1])
+    trust[...] = jnp.where(down == 0, first, jnp.where(across == 0, norm[2], norm[3]))
+    for copy, src, dst in ((came[0], pool_in, pooled), (came[1], grad_in, image_grad)):
+        copy.wait()
+        cl = src.shape[0] // batch
+        for j in range(src.shape[1] // LANES):
+            lanes = slice(j * LANES, (j + 1) * LANES)
+            wide[j] = src[:, lanes].astype(F32)
+            for c in range(cl):
+                dst[c * batch : (c + 1) * batch, lanes] = wide[
+                    j, pl.ds(c, batch, stride=cl), :
+                ].astype(BF16)
+
+
+def final_pass(pooled, image_grad, grad_sum, sums, *small):
+    batch, cl, pixels = image_grad.shape
+    flat = lambda a: a.reshape(a.shape[0] * a.shape[1], a.shape[2])
+    parts = (flat(pooled), flat(image_grad), grad_sum, sums)
+    student, regress = small[0:2]
+    outs = [jax.ShapeDtypeStruct((cl * batch, a.shape[2]), BF16) for a in (pooled, image_grad)]
+    for a in (student, regress):
+        outs += [jax.ShapeDtypeStruct(a.shape, F32)] * 4 + [jax.ShapeDtypeStruct(a.shape, BF16)]
+    outs.append(jax.ShapeDtypeStruct((2, 2), F32))
+    vmem = pl.BlockSpec(memory_space=pltpu.VMEM)
+    results = pl.pallas_call(
+        functools.partial(final_kernel, batch),
+        out_shape=outs,
+        in_specs=[pl.BlockSpec(memory_space=pl.ANY)] * 4 + [vmem] * len(small),
+        out_specs=[vmem] * len(outs),
+        scratch_shapes=[pltpu.VMEM(a.shape, a.dtype) for a in parts]
+        + [
+            pltpu.VMEM((pixels // LANES, batch * cl, LANES), F32),
+            pltpu.SemaphoreType.DMA((len(parts),)),
+        ],
+        compiler_params=pltpu.CompilerParams(vmem_limit_bytes=58 << 20),
+        name="final",
+    )(*parts, *small)
+    acts = [a.reshape(cl, batch, a.shape[1]) for a in results[0:2]]
+    return (*acts, *(a.T for a in results[2:12]), results[12])
+
+
 def split_pieces(weights):
     rows, cols = weights.shape
     return weights.reshape(rows, cols // 2, 2).transpose(2, 1, 0).reshape(cols, rows)
@@ -723,34 +811,21 @@
         mask=hint_mask,
     )
     if fused:
-        arrays.update(
-            student_master=student_master,
-            regress_master=regress_master,
-            teacher=teacher_weight,
-            mom_student=mom_student,
-            sq_student=sq_student,
-            mom_regress=mom_regress,
-            sq_regress=sq_regress,
-        )
-        pooled, image_grad, grad_sum, sums = layer_pass(n, group, fused, arrays)
-        souts, regs = student_master.shape[1], regress_master.shape[1]
-        student_grad = grad_sum[:, 0:souts]
-        regress_grad = grad_sum[:, souts : souts + regs]
-    else:
-        arrays.update(gathered_filters(student_master, regress_master, teacher_weight))
-        pooled, image_grad, student_part, regress_part = layer_pass(n, group, fused, arrays)
-        student_grad, regress_grad = scattered_grads(student_part, regress_part)
+        small = (student_master, regress_master, mom_student, sq_student, mom_regress, sq_regress)
+        small = [a.T for a in small]
+        names = ("student_t", "regress_t", "mom_student", "sq_student", "mom_regress", "sq_regress")
+        arrays.update(zip(names, small))
+        parts = layer_pass(n, group, fused, dict(arrays, teacher_t=teacher_weight.T))
+        return final_pass(*parts, *small, ema_student.T, ema_regress.T)
+    arrays.update(gathered_filters(student_master, regress_master, teacher_weight))
+    pooled, image_grad, student_part, regress_part = layer_pass(n, group, fused, arrays)
+    student_grad, regress_grad = scattered_grads(student_part, regress_part)
     mom_s, sq_s, upd_s = lamb_update(student_master, student_grad, mom_student, sq_student)
     mom_r, sq_r, upd_r = lamb_update(regress_master, regress_grad, mom_regress, sq_regress)
-    if fused:
-        all_sums = sums[0, 0:4]
-    else:
-        all_sums = lax.psum(
-            jnp.stack(
-                [jnp.sum(v * v) for v in (student_master, upd_s, regress_master, upd_r)]
-            ),
-            ("dp", "chan"),
-        )
+    all_sums = lax.psum(
+        jnp.stack([jnp.sum(v * v) for v in (student_master, upd_s, regress_master, upd_r)]),
+        ("dp", "chan"),
+    )
     norms = jnp.sqrt(all_sums)
     new_student = student_master - LEARN_RATE * (norms[0] / norms[1]) * upd_s
     new_regress = regress_master - LEARN_RATE * (norms[2] / norms[3]) * upd_r

time: 189 us -> 158 us (0.84)
  local copies, waits for them, and re-layouts: 22.8 us -> 0 us
  Pallas kernels: 160 us -> 157 us
  between operations: 3.48 us -> 0.65 us
  other arithmetic: 2.01 us -> 0 us
    unnamed x41 -> x0, local copies, waits for them, and re-layouts: 20.8 us -> none
    pallas_call x1, Pallas kernels: 160 us -> 152 us  [layer_pass(): pl.pallas_call(functools.partial(layer_kernel, size, names), out_shape=li...]
    pallas_call x0 -> x1, Pallas kernels: none -> 5.4 us  [final_pass(): pl.pallas_call(functools.partial(final_kernel, batch), out_shape=outs, in...]
    convert_element_type x2 -> x0, other arithmetic: 1.99 us -> none  [the longest x1 1.03 us: on_device(): new_regress.astype(BF16)]
where the time goes in v3:
time: 158 us
  Pallas kernels  157 us (99%)
    pallas_call x1, Pallas kernels, layer_pass(): pl.pallas_call(functools.partial(layer_kernel, size, names), out_shape=li...  152 us
    pallas_call x1, Pallas kernels, final_pass(): pl.pallas_call(functools.partial(final_kernel, batch), out_shape=outs, in...  5.4 us

profile of v3, /device:TPU:0, one launch (start us, length us, event | category | flops | bytes accessed | tf_op | source)
XLA Modules:
  0.0 157.6 jit_solution(7314405857000429470)
XLA Ops:
  0.6 151.5 %layer.1 = (bf16[16,32,256]{2,1,0:T(8,128)(2,1)}, bf16[16,32,1024]{2,1,0:T(8,128)(2,1)}, f32[128,144]{1,0:T(8,128)}, f32[8,128]{1,0:T(8,128)}) custom-call(bf16[512,1024]{1,0:T(8,128)(2,1)} %bitcast.46, s32[512,1024]{1,0:T(8,128)} %bitcast.45, s32[768,1024]{1,0:T(8,128)} %bitcast.44, s32[512,256]{1,0:T(8,128)} %bitcast.48, bf16[512,256]{1,0:T(8,128)(2,1)} %bitcast.49, ...), custom_call_target="tpu_custom_call" | custom-call | flops 16307453952 | bytes 16777216 | tf_op jit(solution)/shard_map/layer/pallas_call | solution.py:663
  152.2 5.4 %final.1 = (bf16[512,256]{1,0:T(8,128)(2,1)}, bf16[512,1024]{1,0:T(8,128)(2,1)}, f32[64,144]{1,0:T(8,128)}, f32[64,144]{1,0:T(8,128)}, f32[64,144]{1,0:T(8,128)}...) custom-call(bf16[512,256]{1,0:T(8,128)(2,1)} %bitcast.29, ...), custom_call_target="tpu_custom_call" | custom-call | tf_op jit(solution)/shard_map/final/pallas_call | solution.py:731

commit v4 on v3

--- a/solution.py
+++ b/solution.py
@@ -21,8 +21,11 @@
 MESH = pl.DeviceIdType.MESH
 F32 = jnp.float32
 BF16 = jnp.bfloat16
-CHUNK = 256
+STAGES = 1
+CHUNK = IMG * IMG // STAGES
 LANES = 128
+AHEAD = 3
+EARLY = 2
 
 
 def dot(left, right):
@@ -128,24 +131,43 @@
     for j in range(r.cot_wide.shape[0]):
         r.cot_wide[j] = r.raw_cot[:, j * LANES : (j + 1) * LANES].astype(F32)
 
-    def in_copies(slot, step):
+    def in_copies(slot, step, part):
         to = beside(step)
-        return (
+        rows = pl.ds(0, 2 * cl) if part == 0 else pl.ds(2 * cl, tl)
+        copies = [
             remote(
-                send.at[slot, to],
-                held.at[slot, me],
-                r.in_send.at[slot, step],
-                r.in_recv.at[slot, step],
+                send.at[slot, to, rows],
+                held.at[slot, me, rows],
+                r.in_send.at[slot, part, step],
+                r.in_recv.at[slot, part, step],
                 at_chan(to),
-            ),
-            remote(
-                r.send_pool.at[slot, to],
-                r.held_pool.at[slot, me],
-                r.pool_in_send.at[slot, step],
-                r.pool_in_recv.at[slot, step],
-                at_chan(to),
-            ),
-        )
+            )
+        ]
+        if part == 1:
+            copies.append(
+                remote(
+                    r.send_pool.at[slot, to],
+                    r.held_pool.at[slot, me],
+                    r.pool_in_send.at[slot, step],
+                    r.pool_in_recv.at[slot, step],
+                    at_chan(to),
+                )
+            )
+        return copies
+
+    def start_in(slot, part):
+        for step in range(1, n):
+            for copy in in_copies(slot, step, part):
+                copy.start()
+
+    def wait_in(slot, part):
+        for step in range(1, n):
+            for copy in in_copies(slot, step, part):
+                copy.wait_recv()
+
+    def start_later(slot, part):
+        later = slot + (part + AHEAD) // 2
+        pl.when(later < slots)(lambda: start_in(later, (part + AHEAD) % 2))
 
     def own_copies(slot):
         return (
@@ -193,8 +215,10 @@
             for copy in out_copies(slot, step):
                 copy.start()
 
-    def start_early():
-        for slot in range(slots - 1):
+    out_order = {"early": range(0, EARLY), "mid": range(EARLY, slots - 1), "late": range(slots - 1, slots)}
+
+    def start_outs(when):
+        for slot in out_order[when]:
             start_out(slot)
 
     def prepare(slot, carry):
@@ -211,9 +235,8 @@
                     dst[slot, to, first : first + rows, j * LANES : (j + 1) * LANES] = (
                         src[j, pl.ds(first_row, rows, stride=batch), :].astype(F32).astype(BF16)
                     )
-        for step in range(1, n):
-            for copy in in_copies(slot, step):
-                copy.start()
+        for part in range(2):
+            pl.when(2 * slot + part < AHEAD)(functools.partial(start_in, slot, part))
         for copy in own_copies(slot):
             copy.start()
         return carry
@@ -302,9 +325,10 @@
             r.w_in_back[:, tap * 2 * chans : (tap + 1) * 2 * chans] = total[:, 0 : 2 * chans]
             r.w_reg_back[:, tap * regs : (tap + 1) * regs] = total[:, 2 * chans : 2 * chans + regs]
 
-    def columns(load, rows, dst):
-        def group(g, carry):
-            first = pl.multiple_of(g * 16, 16)
+    def columns(load, rows, dst, stage):
+        many = rows // (16 * STAGES)
+        for g in range(many):
+            first = pl.multiple_of((stage * many + g) * 16, 16)
             base = load(first)
             for ky in range(3):
                 if ky == 1:
@@ -319,16 +343,29 @@
                         tap = pltpu.roll(moved, (pixels - (kx - 1)) % pixels, 1)
                         tap = tap * r.edge[2 if kx == 0 else 3]
                     dst[pl.ds((3 * ky + kx) * rows + first, 16), :] = tap
+
+    def stages(*bodies):
+        def one(stage, carry):
+            for body in bodies:
+                body(stage)
             return carry
 
-        lax.fori_loop(0, rows // 16, group, 0, unroll=2)
+        lax.fori_loop(0, STAGES, one, 0)
 
     def chunks(body):
-        def one(c, carry):
-            body(pl.ds(pl.multiple_of(c * CHUNK, CHUNK), CHUNK))
-            return carry
-
-        lax.fori_loop(0, pixels // CHUNK, one, 0)
+        def one(stage):
+            body(pl.ds(pl.multiple_of(stage * CHUNK, CHUNK), CHUNK))
+
+        return one
+
+    def add_grads(grads, left, right):
+        many = grads.shape[0] // STAGES
+
+        def one(stage):
+            rows = pl.ds(pl.multiple_of(stage * many, 16), many)
+            grads[rows, :] += dot_nt(left[rows, :], right[...])
+
+        return one
 
     def corner_of(here):
         at = lax.broadcasted_iota(jnp.int32, (1, CHUNK), 1)
@@ -389,88 +426,112 @@
                 at_chan(beside(step)),
             )
 
+    def step_chip(which):
+        grads, _, came, out, _ = parts[which]
+        cols = slice(2 * chans, 2 * chans + regs) if which == 0 else slice(0, 2 * chans)
+        core_copy(which).wait_recv()
+        for step in range(1, pairs):
+            to = lax.rem(chip + step, pairs)
+            out[step] = (grads[block(2 * to + core), :] + came[to].astype(F32)).astype(BF16)
+            chip_copy(which, step).start()
+        r.whole_grad[:, cols] = grads[block(row), :] + came[chip].astype(F32)
+
     def image(slot, carry):
-        for step in range(1, n):
-            for copy in in_copies(slot, step):
-                copy.wait_recv()
+        last = slot == slots - 1
+        wait_in(slot, 0)
+        start_later(slot, 0)
         for copy in own_copies(slot):
             copy.wait()
-        pl.when(slot == slots - 1)(start_early)
 
         def image_rows(first):
             return held[slot, first // cl, pl.ds(pl.multiple_of(first % cl, 16), 16), :]
 
-        columns(image_rows, chans, r.x_cols)
-        r.pool_part[slot] = jnp.zeros((chans, cells), BF16)
+        def picked(here):
+            return held[slot, :, cl : 2 * cl, here].reshape(chans, CHUNK).astype(F32) > 0.5
 
         def head(here):
             pre = dot(r.w_in[0 : 2 * chans, :], r.x_cols[:, here])
-            pick = held[slot, :, cl : 2 * cl, here].reshape(chans, CHUNK).astype(F32)
-            value = jnp.where(pick > 0.5, pre[chans:], pre[:chans]).astype(BF16)
-            r.out_low[:, here] = value
+            r.out_low[:, here] = jnp.where(picked(here), pre[chans:], pre[:chans]).astype(BF16)
+
+        def teach(here):
+            r.teach[:, here] = dot(r.w_in[2 * chans :, :], r.x_cols[:, here])
+
+        def guess(here):
+            r.guess[:, here] = dot(r.w_reg[...], r.o_cols[:, here])
+
+        def pooling(here):
             cell_win = r.held_pool[slot, :, 0:cl, :].reshape(chans, cells)
             cell_cot = r.held_pool[slot, :, cl : 2 * cl, :].reshape(chans, cells)
             chosen = dot(cell_win, r.up[:, here]) == corner_of(here)
             spread = dot(cell_cot, r.up[:, here])
             r.pool_back[:, here] = jnp.where(chosen, spread, 0.0).astype(BF16)
-            kept = jnp.where(chosen, value.astype(F32), 0.0).astype(BF16)
+            kept = jnp.where(chosen, r.out_low[:, here].astype(F32), 0.0).astype(BF16)
             part = dot_nt(kept, r.up[:, here])
             r.pool_part[slot] = (r.pool_part[slot].astype(F32) + part).astype(BF16)
 
-        chunks(head)
-        columns(lambda first: r.out_low[pl.ds(first, 16), :], chans, r.o_cols)
+        def hints(here):
+            pick = held[slot, :, 2 * cl :, here].reshape(touts, CHUNK).astype(F32)
+            target = jnp.where(pick > 0.5, r.teach[touts:, here], r.teach[:touts, here])
+            weight = scale * r.mask[pl.ds(me * slots + slot, 1), here].astype(F32)
+            r.hint[:, here] = (weight * (r.guess[:, here] - target)).astype(BF16)
+
+        def back(here):
+            total = dot(r.w_reg_back[...], r.h_cols[:, here]) + r.pool_back[:, here].astype(F32)
+            pick = picked(here)
+            r.pre_grad[0:chans, here] = jnp.where(pick, 0.0, total).astype(BF16)
+            r.pre_grad[chans:, here] = jnp.where(pick, total, 0.0).astype(BF16)
+
+        def image_back(here):
+            r.low_part[slot, :, here] = dot(r.w_in_back[...], r.p_cols[:, here]).astype(BF16)
+
+        def columns_of(src, dst):
+            rows = src.shape[0]
+            return lambda stage: columns(lambda first: src[pl.ds(first, 16), :], rows, dst, stage)
 
         spot_mask = r.mask[pl.ds(me * slots + slot, 1), :].astype(F32)
         count = jnp.sum(spot_mask, axis=1, keepdims=True)
         scale = HINT_WEIGHT * (pixels / count)
-
-        def hints(here):
-            teach = dot(r.w_in[2 * chans :, :], r.x_cols[:, here])
-            pick = held[slot, :, 2 * cl :, here].reshape(touts, CHUNK).astype(F32)
-            target = jnp.where(pick > 0.5, teach[touts:], teach[:touts])
-            guess = dot(r.w_reg[...], r.o_cols[:, here])
-            weight = scale * r.mask[pl.ds(me * slots + slot, 1), here].astype(F32)
-            r.hint[:, here] = (weight * (guess - target)).astype(BF16)
-
-        chunks(hints)
-        columns(lambda first: r.hint[pl.ds(first, 16), :], regs, r.h_cols)
-        r.rgrad[...] += dot_nt(r.o_cols[...], r.hint[...])
+        r.pool_part[slot] = jnp.zeros((chans, cells), BF16)
+
+        stages(lambda stage: columns(image_rows, chans, r.x_cols, stage))
+        stages(chunks(head))
+        stages(chunks(teach), columns_of(r.out_low, r.o_cols))
+        stages(chunks(guess))
+        wait_in(slot, 1)
+        start_later(slot, 1)
+        pl.when(last)(lambda: start_outs("early"))
+        stages(chunks(hints))
+        stages(add_grads(r.rgrad, r.o_cols, r.hint), columns_of(r.hint, r.h_cols))
         if fused:
-            pl.when(slot == slots - 1)(lambda: start_core(0))
-
-        def back(here):
-            total = dot(r.w_reg_back[...], r.h_cols[:, here]) + r.pool_back[:, here].astype(F32)
-            pick = held[slot, :, cl : 2 * cl, here].reshape(chans, CHUNK).astype(F32) > 0.5
-            r.pre_grad[0:chans, here] = jnp.where(pick, 0.0, total).astype(BF16)
-            r.pre_grad[chans:, here] = jnp.where(pick, total, 0.0).astype(BF16)
-
-        chunks(back)
-        columns(lambda first: r.pre_grad[pl.ds(first, 16), :], 2 * chans, r.p_cols)
-        r.sgrad[...] += dot_nt(r.x_cols[...], r.pre_grad[...])
+            pl.when(last)(lambda: start_core(0))
+        stages(chunks(pooling))
+        stages(chunks(back))
+        stages(add_grads(r.sgrad, r.x_cols, r.pre_grad), columns_of(r.pre_grad, r.p_cols))
         if fused:
-            pl.when(slot == slots - 1)(lambda: start_core(1))
-
-        def image_back(here):
-            r.low_part[slot, :, here] = dot(r.w_in_back[...], r.p_cols[:, here]).astype(BF16)
-
-        chunks(image_back)
-        pl.when(slot == slots - 1)(lambda: start_out(slots - 1))
+
+            def reduce_more():
+                start_core(1)
+                step_chip(0)
+
+            pl.when(last)(reduce_more)
+        stages(chunks(image_back))
+        if not fused:
+
+            def start_rest():
+                start_outs("mid")
+                start_outs("late")
+
+            pl.when(last)(start_rest)
         for copy in own_out(slot):
             copy.start()
         return carry
 
+    if fused:
+        r.whole_grad[...] = jnp.zeros_like(r.whole_grad)
     lax.fori_loop(0, slots, image, 0)
 
     if fused:
-        r.whole_grad[...] = jnp.zeros_like(r.whole_grad)
-        for which, cols in ((0, slice(2 * chans, 2 * chans + regs)), (1, slice(0, 2 * chans))):
-            grads, _, came, out, _ = parts[which]
-            core_copy(which).wait_recv()
-            for step in range(1, pairs):
-                to = lax.rem(chip + step, pairs)
-                out[step] = (grads[block(2 * to + core), :] + came[to].astype(F32)).astype(BF16)
-                chip_copy(which, step).start()
-            r.whole_grad[:, cols] = grads[block(row), :] + came[chip].astype(F32)
+        step_chip(1)
         for which, cols in ((0, slice(2 * chans, 2 * chans + regs)), (1, slice(0, 2 * chans))):
             came = parts[which][4]
             for step in range(1, pairs):
@@ -483,6 +544,7 @@
         for step in range(1, n):
             r.zs_send[step] = dot_nt(low_grad, r.spread[beside(step)]).astype(BF16)
             chan_copy(step).start()
+        start_outs("mid")
         total = dot_nt(
             r.whole_grad[...], r.spread[me].astype(F32), precision=lax.Precision.HIGHEST
         )
@@ -503,6 +565,15 @@
         for index, value in enumerate((student, upd_s, regress, upd_r)):
             square = jnp.sum(jnp.sum(value * value, axis=1, keepdims=True), axis=0, keepdims=True)
             tile = jnp.where(place == index, square, tile)
+        r.part_chans[me] = tile
+        for step in range(1, n):
+            chan_norm(step).start()
+        start_outs("late")
+        for step in range(1, n):
+            chan_norm(step).wait_recv()
+        tile = r.part_chans[0]
+        for index in range(1, n):
+            tile += r.part_chans[index]
         r.part_rows[row] = tile
         for step in range(1, group):
             row_norm(step).start()
@@ -511,19 +582,11 @@
         tile = r.part_rows[0]
         for index in range(1, group):
             tile += r.part_rows[index]
-        r.part_chans[me] = tile
-        for step in range(1, n):
-            chan_norm(step).start()
-        for step in range(1, n):
-            chan_norm(step).wait_recv()
-        tile = r.part_chans[0]
-        for index in range(1, n):
-            tile += r.part_chans[index]
         r.sums[...] = tile
 
     def finish(slot, carry):
         for step in range(1, n):
-            for copy in in_copies(slot, step):
+            for copy in in_copies(slot, step, 0) + in_copies(slot, step, 1):
                 copy.wait_send()
             for copy in out_copies(slot, step):
                 copy.wait()
@@ -606,11 +669,15 @@
         "out_low": pltpu.VMEM((chans, pixels), BF16),
         "pool_back": pltpu.VMEM((chans, pixels), BF16),
         "hint": pltpu.VMEM((regs, pixels), BF16),
+        "teach": pltpu.VMEM((2 * touts, pixels), F32),
+        "guess": pltpu.VMEM((regs, pixels), F32),
         "pre_grad": pltpu.VMEM((2 * chans, pixels), BF16),
         "own_sem": dma(slots, 2),
         "own_out_sem": dma(slots, 2),
     }
-    for name in ("in", "pool_in", "out", "pool_out"):
+    scratch["in_send"] = dma(slots, 2, n)
+    scratch["in_recv"] = dma(slots, 2, n)
+    for name in ("pool_in", "out", "pool_out"):
         scratch[name + "_send"] = dma(slots, n)
         scratch[name + "_recv"] = dma(slots, n)
     if fused:

time: 158 us -> 147 us (0.930)
  Pallas kernels: 157 us -> 146 us
    pallas_call x1, Pallas kernels: 152 us -> 141 us  [layer_pass(): pl.pallas_call(functools.partial(layer_kernel, size, names), out_shape=li...]
where the time goes in v4:
time: 147 us
  Pallas kernels  146 us (99%)
    pallas_call x1, Pallas kernels, layer_pass(): pl.pallas_call(functools.partial(layer_kernel, size, names), out_shape=li...  141 us
    pallas_call x1, Pallas kernels, final_pass(): pl.pallas_call(functools.partial(final_kernel, batch), out_shape=outs, in...  5.4 us

profile of v4, /device:TPU:0, one launch (start us, length us, event | category | flops | bytes accessed | tf_op | source)
XLA Modules:
  0.0 147.0 jit_solution(9923493844791566770)
XLA Ops:
  0.6 140.8 %layer.1 = (bf16[16,32,256]{2,1,0:T(8,128)(2,1)}, bf16[16,32,1024]{2,1,0:T(8,128)(2,1)}, f32[128,144]{1,0:T(8,128)}, f32[8,128]{1,0:T(8,128)}) custom-call(bf16[512,1024]{1,0:T(8,128)(2,1)} %bitcast.46, s32[512,1024]{1,0:T(8,128)} %bitcast.45, s32[768,1024]{1,0:T(8,128)} %bitcast.44, s32[512,256]{1,0:T(8,128)} %bitcast.48, bf16[512,256]{1,0:T(8,128)(2,1)} %bitcast.49, ...), custom_call_target="tpu_custom_call" | custom-call | flops 16307453952 | bytes 16777216 | tf_op jit(solution)/shard_map/layer/pallas_call | solution.py:730
  141.5 5.4 %final.1 = (bf16[512,256]{1,0:T(8,128)(2,1)}, bf16[512,1024]{1,0:T(8,128)(2,1)}, f32[64,144]{1,0:T(8,128)}, f32[64,144]{1,0:T(8,128)}, f32[64,144]{1,0:T(8,128)}...) custom-call(bf16[512,256]{1,0:T(8,128)(2,1)} %bitcast.29, ...), custom_call_target="tpu_custom_call" | custom-call | tf_op jit(solution)/shard_map/final/pallas_call | solution.py:798

commit v5 on v4

--- a/solution.py
+++ b/solution.py
@@ -24,8 +24,12 @@
 STAGES = 1
 CHUNK = IMG * IMG // STAGES
 LANES = 128
-AHEAD = 3
-EARLY = 2
+AHEAD = 5
+ORDER = (2, 1, 3)
+EARLY = 3
+LOADS = 1
+CHIP_AT = 1
+PIECES = 4
 
 
 def dot(left, right):
@@ -45,6 +49,11 @@
 
 def layer_kernel(size, names, *refs):
     r = types.SimpleNamespace(**dict(zip(names, refs)))
+    small_loads = []
+    for index, name in enumerate(size["small"]):
+        small_loads.append(
+            pltpu.make_async_copy(getattr(r, name + "_hbm"), getattr(r, name), r.small_sem.at[index])
+        )
     n, batch, cl, tl, rl = size["n"], size["batch"], size["cl"], size["tl"], size["rl"]
     fused, group = size["fused"], size["group"]
     slots = batch // n
@@ -57,7 +66,16 @@
     held, send = r.held, r.send
 
     def beside(step):
-        return lax.rem(me + step, n)
+        if n & (n - 1):
+            return lax.rem(me + step, n)
+        other, bit = me, 1
+        while bit < n:
+            if step & bit:
+                other = other + bit - 2 * bit * ((me // bit) % 2)
+            bit *= 2
+        return other
+
+    partners = ORDER if n == 4 else range(1, n)
 
     def at_chan(index):
         return {"chan": index}
@@ -74,19 +92,37 @@
     if fused:
         greeted += [at_row(lax.rem(row + step, group)) for step in range(1, group)]
 
-    loads = [
-        pltpu.make_async_copy(r.images, r.raw, r.load_sem.at[0]),
-        pltpu.make_async_copy(r.cot, r.raw_cot, r.load_sem.at[1]),
-    ]
-    for src, dst in ((r.swin, r.swin_wide), (r.twin, r.twin_wide), (r.pwin, r.pwin_wide)):
-        for j in range(dst.shape[0]):
-            loads.append(
-                pltpu.make_async_copy(
-                    src.at[:, pl.ds(j * LANES, LANES)], dst.at[j], r.load_sem.at[len(loads)]
-                )
-            )
-    for copy in loads:
+    sources = {
+        "images": (r.images, r.raw, None),
+        "swin": (r.swin, r.swin_wide, LANES),
+        "twin": (r.twin, r.twin_wide, LANES),
+        "pwin": (r.pwin, r.pwin_wide, LANES),
+        "cot": (r.cot, r.raw_cot, None),
+    }
+    loads, count = {}, 0
+    for name, (src, dst, lanes) in sources.items():
+        loads[name] = []
+        for j in range(dst.shape[0] if lanes else 1):
+            pair = (src.at[:, pl.ds(j * LANES, LANES)], dst.at[j]) if lanes else (src, dst)
+            loads[name].append(pltpu.make_async_copy(*pair, r.load_sem.at[count]))
+            count += 1
+
+    def start_load(*names):
+        for name in names:
+            for copy in loads[name]:
+                copy.start()
+
+    if LOADS == 0:
+        start_load(*sources)
+    else:
+        start_load("images", "swin")
+
+    for copy in small_loads:
         copy.start()
+
+    def wait_load(name):
+        for copy in loads[name]:
+            copy.wait()
 
     barrier = pltpu.get_barrier_semaphore()
     for device in greeted:
@@ -99,18 +135,6 @@
             return pl.ds(pl.multiple_of(index * depth, 16), depth)
 
         mine = block(row)
-        r.flat[...] = jnp.zeros_like(r.flat)
-        r.flat[0 : 2 * cl, 0:depth] = r.student_t[...]
-        r.flat[2 * cl : 2 * cl + rl, 0:depth] = r.regress_t[...]
-        r.filters[me, mine, 0:LANES] = r.flat[...].T[0:depth, :].astype(BF16)
-        r.teach_flat[...] = jnp.zeros_like(r.teach_flat)
-        r.teach_flat[0 : 2 * tl, :] = r.teacher_t[...].astype(F32)
-        r.teach_cols[...] = r.teach_flat[...].T
-        r.filters[me, mine, LANES:] = r.teach_cols[mine, :].astype(BF16)
-
-    pl.semaphore_wait(barrier, len(greeted))
-
-    if fused:
         filter_z = [
             remote(
                 r.filters.at[me, mine],
@@ -121,15 +145,15 @@
             )
             for step in range(1, n)
         ]
-        for copy in filter_z:
-            copy.start()
-
-    for copy in loads:
-        copy.wait()
-    for j in range(r.wide.shape[0]):
-        r.wide[j] = r.raw[:, j * LANES : (j + 1) * LANES].astype(F32)
-    for j in range(r.cot_wide.shape[0]):
-        r.cot_wide[j] = r.raw_cot[:, j * LANES : (j + 1) * LANES].astype(F32)
+        if n == 4:
+            passed = beside(2)
+            filter_z[2] = remote(
+                r.filters.at[passed, mine],
+                r.filters.at[passed, mine],
+                r.fz_send.at[3],
+                r.fz_recv.at[3],
+                at_chan(beside(1)),
+            )
 
     def in_copies(slot, step, part):
         to = beside(step)
@@ -156,12 +180,12 @@
         return copies
 
     def start_in(slot, part):
-        for step in range(1, n):
+        for step in partners:
             for copy in in_copies(slot, step, part):
                 copy.start()
 
     def wait_in(slot, part):
-        for step in range(1, n):
+        for step in partners:
             for copy in in_copies(slot, step, part):
                 copy.wait_recv()
 
@@ -185,14 +209,14 @@
         return (
             remote(
                 r.low_part.at[slot, lanes_of(to)],
-                r.grad_out.at[me * slots + slot],
+                r.grad_land.at[me * slots + slot],
                 r.out_send.at[slot, step],
                 r.out_recv.at[slot, step],
                 at_chan(to),
             ),
             remote(
                 r.pool_part.at[slot, lanes_of(to)],
-                r.pool_out.at[me * slots + slot],
+                r.pool_land.at[me * slots + slot],
                 r.pool_out_send.at[slot, step],
                 r.pool_out_recv.at[slot, step],
                 at_chan(to),
@@ -203,17 +227,29 @@
         here = me * slots + slot
         return (
             pltpu.make_async_copy(
-                r.low_part.at[slot, lanes_of(me)], r.grad_out.at[here], r.own_out_sem.at[slot, 0]
+                r.low_part.at[slot, lanes_of(me)], r.grad_land.at[here], r.own_out_sem.at[slot, 0]
             ),
             pltpu.make_async_copy(
-                r.pool_part.at[slot, lanes_of(me)], r.pool_out.at[here], r.own_out_sem.at[slot, 1]
+                r.pool_part.at[slot, lanes_of(me)], r.pool_land.at[here], r.own_out_sem.at[slot, 1]
             ),
         )
 
     def start_out(slot):
-        for step in range(1, n):
+        for step in partners:
             for copy in out_copies(slot, step):
                 copy.start()
+
+    def land(slot):
+        for step in partners:
+            for copy in out_copies(slot, step):
+                copy.wait_recv()
+        for copy in own_out(slot):
+            copy.wait()
+        for src, dst in ((r.grad_land, r.wide), (r.pool_land, r.cot_wide)):
+            for z in range(n):
+                for j in range(dst.shape[0]):
+                    part = src[z * slots + slot, :, j * LANES : (j + 1) * LANES].astype(F32)
+                    dst[j, pl.ds(z * slots + slot, cl, stride=batch), :] = part
 
     out_order = {"early": range(0, EARLY), "mid": range(EARLY, slots - 1), "late": range(slots - 1, slots)}
 
@@ -221,27 +257,65 @@
         for slot in out_order[when]:
             start_out(slot)
 
-    def prepare(slot, carry):
-        for to in range(n):
-            first_row = to * slots + slot
-            for src, dst, first, rows in (
-                (r.wide, send, 0, cl),
-                (r.swin_wide, send, cl, cl),
+    def prepare(slot, part):
+        if part == 0:
+            pieces = ((r.wide, send, 0, cl), (r.swin_wide, send, cl, cl))
+        else:
+            pieces = (
                 (r.twin_wide, send, 2 * cl, tl),
                 (r.pwin_wide, r.send_pool, 0, cl),
                 (r.cot_wide, r.send_pool, cl, cl),
-            ):
+            )
+        for to in range(n):
+            first_row = to * slots + slot
+            for src, dst, first, rows in pieces:
                 for j in range(src.shape[0]):
                     dst[slot, to, first : first + rows, j * LANES : (j + 1) * LANES] = (
                         src[j, pl.ds(first_row, rows, stride=batch), :].astype(F32).astype(BF16)
                     )
+
+    def prepare_slot(slot, carry):
         for part in range(2):
+            prepare(slot, part)
             pl.when(2 * slot + part < AHEAD)(functools.partial(start_in, slot, part))
         for copy in own_copies(slot):
             copy.start()
         return carry
 
-    lax.fori_loop(0, slots, prepare, 0)
+    for copy in small_loads:
+        copy.wait()
+    wait_load("images")
+    for j in range(r.wide.shape[0]):
+        r.wide[j] = r.raw[:, j * LANES : (j + 1) * LANES].astype(F32)
+    wait_load("swin")
+    if LOADS == 1:
+        start_load("twin", "pwin", "cot")
+    prepare(0, 0)
+    pl.semaphore_wait(barrier, len(greeted))
+    start_in(0, 0)
+    if fused:
+        r.flat[...] = jnp.zeros_like(r.flat)
+        r.flat[0 : 2 * cl, 0:depth] = r.student_t[...]
+        r.flat[2 * cl : 2 * cl + rl, 0:depth] = r.regress_t[...]
+        r.filters[me, mine, 0:LANES] = r.flat[...].T[0:depth, :].astype(BF16)
+        r.teach_flat[...] = jnp.zeros_like(r.teach_flat)
+        r.teach_flat[0 : 2 * tl, :] = r.teacher_t[...].astype(F32)
+        r.teach_cols[...] = r.teach_flat[...].T
+        r.filters[me, mine, LANES:] = r.teach_cols[mine, :].astype(BF16)
+        for copy in filter_z[:2] if n == 4 else filter_z:
+            copy.start()
+    for name in ("twin", "pwin", "cot"):
+        wait_load(name)
+    for j in range(r.cot_wide.shape[0]):
+        r.cot_wide[j] = r.raw_cot[:, j * LANES : (j + 1) * LANES].astype(F32)
+    prepare(0, 1)
+    start_in(0, 1)
+    for copy in own_copies(0):
+        copy.start()
+    if fused and n == 4:
+        filter_z[1].wait_recv()
+        filter_z[2].start()
+    lax.fori_loop(1, slots, prepare_slot, 0)
 
     lane = lax.broadcasted_iota(jnp.int32, (16, pixels), 1)
     row_of, col_of = lane // IMG, lane % IMG
@@ -272,7 +346,7 @@
             )
             r.spread[z] = one_hot((LANES, r.spread.shape[2]), col_at, 1)
 
-        for copy in filter_z:
+        for copy in (filter_z[0], filter_z[2]) if n == 4 else filter_z:
             copy.wait_recv()
 
         def filter_chip(step):
@@ -506,12 +580,15 @@
             pl.when(last)(lambda: start_core(0))
         stages(chunks(pooling))
         stages(chunks(back))
+        if fused and CHIP_AT == 1:
+            pl.when(last)(lambda: step_chip(0))
         stages(add_grads(r.sgrad, r.x_cols, r.pre_grad), columns_of(r.pre_grad, r.p_cols))
         if fused:
 
             def reduce_more():
                 start_core(1)
-                step_chip(0)
+                if CHIP_AT == 0:
+                    step_chip(0)
 
             pl.when(last)(reduce_more)
         stages(chunks(image_back))
@@ -541,16 +618,18 @@
                 total += came[step].astype(F32)
             r.whole_grad[:, cols] = total
         low_grad = r.whole_grad[...].astype(BF16)
-        for step in range(1, n):
+        for step in partners:
             r.zs_send[step] = dot_nt(low_grad, r.spread[beside(step)]).astype(BF16)
             chan_copy(step).start()
         start_outs("mid")
         total = dot_nt(
             r.whole_grad[...], r.spread[me].astype(F32), precision=lax.Precision.HIGHEST
         )
-        for step in range(1, n):
+        for slot in out_order["early"]:
+            land(slot)
+        for step in partners:
             chan_copy(step).wait_recv()
-        for step in range(1, n):
+        for step in partners:
             total += r.zs_recv[step].astype(F32)
         r.tall[0:depth, :] = total
         total = r.tall[...].T[:, 0:depth]
@@ -566,10 +645,12 @@
             square = jnp.sum(jnp.sum(value * value, axis=1, keepdims=True), axis=0, keepdims=True)
             tile = jnp.where(place == index, square, tile)
         r.part_chans[me] = tile
-        for step in range(1, n):
+        for step in partners:
             chan_norm(step).start()
         start_outs("late")
-        for step in range(1, n):
+        for slot in out_order["mid"]:
+            land(slot)
+        for step in partners:
             chan_norm(step).wait_recv()
         tile = r.part_chans[0]
         for index in range(1, n):
@@ -584,19 +665,21 @@
             tile += r.part_rows[index]
         r.sums[...] = tile
 
+    for slot in out_order["late"] if fused else range(slots):
+        land(slot)
+    for src, dst in ((r.wide, r.grad_out), (r.cot_wide, r.pool_out)):
+        for j in range(src.shape[0]):
+            dst[:, j * LANES : (j + 1) * LANES] = src[j].astype(BF16)
+
     def finish(slot, carry):
-        for step in range(1, n):
-            for copy in in_copies(slot, step, 0) + in_copies(slot, step, 1):
+        for step in partners:
+            for copy in (*in_copies(slot, step, 0), *in_copies(slot, step, 1), *out_copies(slot, step)):
                 copy.wait_send()
-            for copy in out_copies(slot, step):
-                copy.wait()
-        for copy in own_out(slot):
-            copy.wait()
         return carry
 
     lax.fori_loop(0, slots, finish, 0)
     if fused:
-        for step in range(1, n):
+        for step in partners:
             filter_z[step - 1].wait_send()
             chan_copy(step).wait_send()
             chan_norm(step).wait_send()
@@ -640,9 +723,11 @@
         for name, a in arrays.items()
     }
     outs = {
-        "pool_out": jax.ShapeDtypeStruct((batch, cl, cells), BF16),
-        "grad_out": jax.ShapeDtypeStruct((batch, cl, pixels), BF16),
+        "pool_out": jax.ShapeDtypeStruct((cl * batch, cells), BF16),
+        "grad_out": jax.ShapeDtypeStruct((cl * batch, pixels), BF16),
     }
+    small = tuple(name for name in ins if name not in in_hbm)
+    size["small"] = small
     grads = {"sgrad": (9 * chans, 2 * chans), "rgrad": (9 * chans, regs)}
     dma = lambda *shape: pltpu.SemaphoreType.DMA(shape)
     scratch = {
@@ -660,6 +745,8 @@
         "held_pool": pltpu.VMEM((slots, n, 2 * cl, cells), BF16),
         "low_part": pltpu.VMEM((slots, chans, pixels), BF16),
         "pool_part": pltpu.VMEM((slots, chans, cells), BF16),
+        "pool_land": pltpu.VMEM((batch, cl, cells), BF16),
+        "grad_land": pltpu.VMEM((batch, cl, pixels), BF16),
         "edge": pltpu.VMEM((4, 16, pixels), BF16),
         "up": pltpu.VMEM((cells, pixels), BF16),
         "x_cols": pltpu.VMEM((9 * chans, pixels), BF16),
@@ -726,13 +813,14 @@
     else:
         outs.update({name: jax.ShapeDtypeStruct(shape, F32) for name, shape in grads.items()})
     flops = 2 * slots * pixels * 9 * chans * (3 * 2 * chans + 2 * touts + 3 * regs)
-    names = tuple(ins) + tuple(outs) + tuple(scratch)
+    scratch.update({name: pltpu.VMEM(ins[name].shape, ins[name].dtype) for name in small})
+    scratch["small_sem"] = dma(len(small))
+    in_names = tuple(name + "_hbm" if name in small else name for name in ins)
+    names = in_names + tuple(outs) + tuple(scratch)
     return pl.pallas_call(
         functools.partial(layer_kernel, size, names),
         out_shape=list(outs.values()),
-        in_specs=[
-            pl.BlockSpec(memory_space=pl.ANY) if name in in_hbm else vmem for name in ins
-        ],
+        in_specs=[pl.BlockSpec(memory_space=pl.ANY)] * len(ins),
         out_specs=[vmem] * len(outs),
         scratch_shapes=list(scratch.values()),
         compiler_params=pltpu.CompilerParams(
@@ -743,17 +831,31 @@
     )(*ins.values())
 
 
-def final_kernel(batch, *refs):
-    wide, came_sem = refs[-2:]
-    came = []
-    for index, (src, dst) in enumerate(zip(refs[0:4], refs[-6:-2])):
-        came.append(pltpu.make_async_copy(src, dst, came_sem.at[index]))
-        came[-1].start()
-    pool_in, grad_in, grad_sum, sums = refs[-6:-2]
-    student, regress, mom_s, sq_s, mom_r, sq_r, ema_s, ema_r = refs[4:12]
+def final_kernel(*refs):
+    pool_in, grad_in = refs[0:2]
     pooled, image_grad, new_s, new_r, trust = refs[12], refs[13], refs[14:19], refs[19:24], refs[24]
-    came[2].wait()
-    came[3].wait()
+    held, middle, big_sem, small_sem = refs[25:35], refs[35:37], refs[37], refs[38]
+    big, onward = [], []
+    for index, path in enumerate(((pool_in, middle[0], pooled), (grad_in, middle[1], image_grad))):
+        many = path[0].shape[0] // PIECES
+        for piece in range(PIECES):
+            at = pl.ds(piece * many, many)
+            views = [ref.at[at] for ref in path]
+            sems = [big_sem.at[index, piece, side] for side in range(2)]
+            big.append(pltpu.make_async_copy(views[0], views[1], sems[0]))
+            onward.append(pltpu.make_async_copy(views[1], views[2], sems[1]))
+    small = [
+        pltpu.make_async_copy(src, dst, small_sem.at[index])
+        for index, (src, dst) in enumerate(zip(refs[2:12], held))
+    ]
+    for copy in big + small:
+        copy.start()
+    for copy, after in zip(big, onward):
+        copy.wait()
+        after.start()
+    for copy in small:
+        copy.wait()
+    grad_sum, sums, student, regress, mom_s, sq_s, mom_r, sq_r, ema_s, ema_r = held
     norm = [jnp.sqrt(sums[0:1, k : k + 1]) for k in range(4)]
     souts, regs = student.shape[0], regress.shape[0]
     for weights, grads, moment, second, average, outs, top, bottom in (
@@ -773,43 +875,29 @@
     down = lax.broadcasted_iota(jnp.int32, (2, 2), 0)
     first = jnp.where(across == 0, norm[0], norm[1])
     trust[...] = jnp.where(down == 0, first, jnp.where(across == 0, norm[2], norm[3]))
-    for copy, src, dst in ((came[0], pool_in, pooled), (came[1], grad_in, image_grad)):
+    for copy in onward:
         copy.wait()
-        cl = src.shape[0] // batch
-        for j in range(src.shape[1] // LANES):
-            lanes = slice(j * LANES, (j + 1) * LANES)
-            wide[j] = src[:, lanes].astype(F32)
-            for c in range(cl):
-                dst[c * batch : (c + 1) * batch, lanes] = wide[
-                    j, pl.ds(c, batch, stride=cl), :
-                ].astype(BF16)
 
 
 def final_pass(pooled, image_grad, grad_sum, sums, *small):
-    batch, cl, pixels = image_grad.shape
-    flat = lambda a: a.reshape(a.shape[0] * a.shape[1], a.shape[2])
-    parts = (flat(pooled), flat(image_grad), grad_sum, sums)
     student, regress = small[0:2]
-    outs = [jax.ShapeDtypeStruct((cl * batch, a.shape[2]), BF16) for a in (pooled, image_grad)]
+    outs = [jax.ShapeDtypeStruct(a.shape, BF16) for a in (pooled, image_grad)]
     for a in (student, regress):
         outs += [jax.ShapeDtypeStruct(a.shape, F32)] * 4 + [jax.ShapeDtypeStruct(a.shape, BF16)]
     outs.append(jax.ShapeDtypeStruct((2, 2), F32))
-    vmem = pl.BlockSpec(memory_space=pltpu.VMEM)
+    vmem, hbm = (pl.BlockSpec(memory_space=space) for space in (pltpu.VMEM, pl.ANY))
+    kept = (grad_sum, sums, *small)
     results = pl.pallas_call(
-        functools.partial(final_kernel, batch),
+        final_kernel,
         out_shape=outs,
-        in_specs=[pl.BlockSpec(memory_space=pl.ANY)] * 4 + [vmem] * len(small),
-        out_specs=[vmem] * len(outs),
-        scratch_shapes=[pltpu.VMEM(a.shape, a.dtype) for a in parts]
-        + [
-            pltpu.VMEM((pixels // LANES, batch * cl, LANES), F32),
-            pltpu.SemaphoreType.DMA((len(parts),)),
-        ],
+        in_specs=[hbm] * (2 + len(kept)),
+        out_specs=[hbm] * 2 + [vmem] * (len(outs) - 2),
+        scratch_shapes=[pltpu.VMEM(a.shape, a.dtype) for a in (*kept, pooled, image_grad)]
+        + [pltpu.SemaphoreType.DMA((2, PIECES, 2)), pltpu.SemaphoreType.DMA((len(kept),))],
         compiler_params=pltpu.CompilerParams(vmem_limit_bytes=58 << 20),
         name="final",
-    )(*parts, *small)
-    acts = [a.reshape(cl, batch, a.shape[1]) for a in results[0:2]]
-    return (*acts, *(a.T for a in results[2:12]), results[12])
+    )(pooled, image_grad, *kept)
+    return (*results[0:2], *(a.T for a in results[2:12]), results[12])
 
 
 def split_pieces(weights):
@@ -867,6 +955,8 @@
     sq_regress,
     ema_regress,
 ):
+    image_like = lambda a: a.reshape(images.shape)
+    pool_win_like = lambda a: a.reshape(pool_win.shape)
     depth = student_master.shape[0]
     fused = group % 2 == 0 and depth % 16 == 0
     arrays = dict(
@@ -883,7 +973,8 @@
         names = ("student_t", "regress_t", "mom_student", "sq_student", "mom_regress", "sq_regress")
         arrays.update(zip(names, small))
         parts = layer_pass(n, group, fused, dict(arrays, teacher_t=teacher_weight.T))
-        return final_pass(*parts, *small, ema_student.T, ema_regress.T)
+        results = final_pass(*parts, *small, ema_student.T, ema_regress.T)
+        return (pool_win_like(results[0]), image_like(results[1]), *results[2:])
     arrays.update(gathered_filters(student_master, regress_master, teacher_weight))
     pooled, image_grad, student_part, regress_part = layer_pass(n, group, fused, arrays)
     student_grad, regress_grad = scattered_grads(student_part, regress_part)
@@ -899,8 +990,8 @@
     ema_s = EMA_KEEP * ema_student + (1.0 - EMA_KEEP) * new_student
     ema_r = EMA_KEEP * ema_regress + (1.0 - EMA_KEEP) * new_regress
     return (
-        pooled.transpose(1, 0, 2),
-        image_grad.transpose(1, 0, 2),
+        pool_win_like(pooled),
+        image_like(image_grad),
         new_student,
         mom_s,
         sq_s,

time: 147 us -> 143 us (0.973)
  Pallas kernels: 146 us -> 142 us
    pallas_call x1, Pallas kernels: 141 us -> 138 us  [layer_pass(): pl.pallas_call(functools.partial(layer_kernel, size, names), out_shape=li...]
    pallas_call x1, Pallas kernels: 5.4 us -> 3.27 us  [final_pass(): pl.pallas_call(final_kernel, out_shape=outs, in_specs=[hbm] * (2 + len(ke...]
where the time goes in v5:
time: 143 us; the launch traced here: 142 us
  Pallas kernels  142 us (99%)
    pallas_call x1, Pallas kernels, layer_pass(): pl.pallas_call(functools.partial(layer_kernel, size, names), out_shape=li...  138 us
    pallas_call x1, Pallas kernels, final_pass(): pl.pallas_call(final_kernel, out_shape=outs, in_specs=[hbm] * (2 + len(ke...  3.27 us

profile of v5, /device:TPU:0, one launch (start us, length us, event | category | flops | bytes accessed | tf_op | source)
XLA Modules:
  0.0 142.4 jit_solution(7790597536658170752)
XLA Ops:
  0.6 138.3 %layer.1 = (bf16[512,256]{1,0:T(8,128)(2,1)}, bf16[512,1024]{1,0:T(8,128)(2,1)}, f32[128,144]{1,0:T(8,128)}, f32[8,128]{1,0:T(8,128)}) custom-call(bf16[512,1024]{1,0:T(8,128)(2,1)} %bitcast.42, s32[512,1024]{1,0:T(8,128)} %bitcast.41, s32[768,1024]{1,0:T(8,128)} %bitcast.40, s32[512,256]{1,0:T(8,128)} %bitcast.44, bf16[512,256]{1,0:T(8,128)(2,1)} %bitcast.45, ...), custom_call_target="tpu_custom_call" | custom-call | flops 16307453952 | bytes 16777216 | tf_op jit(solution)/shard_map/layer/pallas_call | solution.py:820
  138.9 3.3 %final.1 = (bf16[512,256]{1,0:T(8,128)(2,1)}, bf16[512,1024]{1,0:T(8,128)(2,1)}, f32[64,144]{1,0:T(8,128)}, f32[64,144]{1,0:T(8,128)}, f32[64,144]{1,0:T(8,128)}...) custom-call(bf16[512,256]{1,0:T(8,128)(2,1)} %get-tuple-element.30.r, ...), custom_call_target="tpu_custom_call" | custom-call | tf_op jit(solution)/shard_map/final/pallas_call | solution.py:890

commit v6 on v5

--- a/solution.py
+++ b/solution.py
@@ -25,11 +25,12 @@
 CHUNK = IMG * IMG // STAGES
 LANES = 128
 AHEAD = 5
+NEAR_LATE = 3
+OUT_AT = 1
 ORDER = (2, 1, 3)
-EARLY = 3
+EARLY = 2
 LOADS = 1
 CHIP_AT = 1
-PIECES = 4
 
 
 def dot(left, right):
@@ -234,8 +235,8 @@
             ),
         )
 
-    def start_out(slot):
-        for step in partners:
+    def start_out(slot, steps=partners):
+        for step in steps:
             for copy in out_copies(slot, step):
                 copy.start()
 
@@ -573,11 +574,14 @@
         stages(chunks(guess))
         wait_in(slot, 1)
         start_later(slot, 1)
-        pl.when(last)(lambda: start_outs("early"))
+        if OUT_AT == 0 or not fused:
+            pl.when(last)(lambda: start_outs("early"))
         stages(chunks(hints))
         stages(add_grads(r.rgrad, r.o_cols, r.hint), columns_of(r.hint, r.h_cols))
         if fused:
             pl.when(last)(lambda: start_core(0))
+            if OUT_AT == 1:
+                pl.when(last)(lambda: start_outs("early"))
         stages(chunks(pooling))
         stages(chunks(back))
         if fused and CHIP_AT == 1:
@@ -587,6 +591,8 @@
 
             def reduce_more():
                 start_core(1)
+                if OUT_AT == 2:
+                    start_outs("early")
                 if CHIP_AT == 0:
                     step_chip(0)
 
@@ -622,6 +628,8 @@
             r.zs_send[step] = dot_nt(low_grad, r.spread[beside(step)]).astype(BF16)
             chan_copy(step).start()
         start_outs("mid")
+        far = [step for step in partners if step > NEAR_LATE]
+        start_out(slots - 1, far)
         total = dot_nt(
             r.whole_grad[...], r.spread[me].astype(F32), precision=lax.Precision.HIGHEST
         )
@@ -647,7 +655,7 @@
         r.part_chans[me] = tile
         for step in partners:
             chan_norm(step).start()
-        start_outs("late")
+        start_out(slots - 1, [step for step in partners if step not in far])
         for slot in out_order["mid"]:
             land(slot)
         for step in partners:
@@ -667,9 +675,9 @@
 
     for slot in out_order["late"] if fused else range(slots):
         land(slot)
-    for src, dst in ((r.wide, r.grad_out), (r.cot_wide, r.pool_out)):
+    for src, out in ((r.wide, r.grad_out), (r.cot_wide, r.pool_out)):
         for j in range(src.shape[0]):
-            dst[:, j * LANES : (j + 1) * LANES] = src[j].astype(BF16)
+            out[:, j * LANES : (j + 1) * LANES] = src[j].astype(BF16)
 
     def finish(slot, carry):
         for step in partners:
@@ -704,7 +712,7 @@
     return (moment_new, second_new, update)
 
 
-def layer_pass(n, group, fused, arrays):
+def layer_pass(n, group, fused, arrays, handed=()):
     cl, batch, pixels = arrays["images"].shape
     tl = arrays["twin"].shape[0]
     cells = arrays["pwin"].shape[2]
@@ -723,8 +731,8 @@
         for name, a in arrays.items()
     }
     outs = {
-        "pool_out": jax.ShapeDtypeStruct((cl * batch, cells), BF16),
-        "grad_out": jax.ShapeDtypeStruct((cl * batch, pixels), BF16),
+        "pool_out": pltpu.VMEM((cl * batch, cells), BF16),
+        "grad_out": pltpu.VMEM((cl * batch, pixels), BF16),
     }
     small = tuple(name for name in ins if name not in in_hbm)
     size["small"] = small
@@ -770,8 +778,9 @@
     if fused:
         cols = 2 * chans + 2 * LANES
         tall = -(-depth // LANES) * LANES
-        outs["grad_sum"] = jax.ShapeDtypeStruct((LANES, depth), F32)
-        outs["sums"] = jax.ShapeDtypeStruct((8, LANES), F32)
+        outs["grad_sum"] = pltpu.VMEM((LANES, depth), F32)
+        outs["sums"] = pltpu.VMEM((8, LANES), F32)
+        outs.update({name: pltpu.VMEM(ins[name].shape, F32) for name in handed})
         scratch.update({name: pltpu.VMEM(shape, F32) for name, shape in grads.items()})
         scratch.update(
             {
@@ -813,7 +822,9 @@
     else:
         outs.update({name: jax.ShapeDtypeStruct(shape, F32) for name, shape in grads.items()})
     flops = 2 * slots * pixels * 9 * chans * (3 * 2 * chans + 2 * touts + 3 * regs)
-    scratch.update({name: pltpu.VMEM(ins[name].shape, ins[name].dtype) for name in small})
+    scratch.update(
+        {name: pltpu.VMEM(ins[name].shape, ins[name].dtype) for name in small if name not in outs}
+    )
     scratch["small_sem"] = dma(len(small))
     in_names = tuple(name + "_hbm" if name in small else name for name in ins)
     names = in_names + tuple(outs) + tuple(scratch)
@@ -834,28 +845,14 @@
 def final_kernel(*refs):
     pool_in, grad_in = refs[0:2]
     pooled, image_grad, new_s, new_r, trust = refs[12], refs[13], refs[14:19], refs[19:24], refs[24]
-    held, middle, big_sem, small_sem = refs[25:35], refs[35:37], refs[37], refs[38]
-    big, onward = [], []
-    for index, path in enumerate(((pool_in, middle[0], pooled), (grad_in, middle[1], image_grad))):
-        many = path[0].shape[0] // PIECES
-        for piece in range(PIECES):
-            at = pl.ds(piece * many, many)
-            views = [ref.at[at] for ref in path]
-            sems = [big_sem.at[index, piece, side] for side in range(2)]
-            big.append(pltpu.make_async_copy(views[0], views[1], sems[0]))
-            onward.append(pltpu.make_async_copy(views[1], views[2], sems[1]))
-    small = [
-        pltpu.make_async_copy(src, dst, small_sem.at[index])
-        for index, (src, dst) in enumerate(zip(refs[2:12], held))
+    big_sem = refs[25]
+    big = [
+        pltpu.make_async_copy(src, dst, big_sem.at[index])
+        for index, (src, dst) in enumerate(((grad_in, image_grad), (pool_in, pooled)))
     ]
-    for copy in big + small:
+    for copy in big:
         copy.start()
-    for copy, after in zip(big, onward):
-        copy.wait()
-        after.start()
-    for copy in small:
-        copy.wait()
-    grad_sum, sums, student, regress, mom_s, sq_s, mom_r, sq_r, ema_s, ema_r = held
+    grad_sum, sums, student, regress, mom_s, sq_s, mom_r, sq_r, ema_s, ema_r = refs[2:12]
     norm = [jnp.sqrt(sums[0:1, k : k + 1]) for k in range(4)]
     souts, regs = student.shape[0], regress.shape[0]
     for weights, grads, moment, second, average, outs, top, bottom in (
@@ -875,7 +872,7 @@
     down = lax.broadcasted_iota(jnp.int32, (2, 2), 0)
     first = jnp.where(across == 0, norm[0], norm[1])
     trust[...] = jnp.where(down == 0, first, jnp.where(across == 0, norm[2], norm[3]))
-    for copy in onward:
+    for copy in big:
         copy.wait()
 
 
@@ -890,13 +887,12 @@
     results = pl.pallas_call(
         final_kernel,
         out_shape=outs,
-        in_specs=[hbm] * (2 + len(kept)),
+        in_specs=[vmem] * (2 + len(kept)),
         out_specs=[hbm] * 2 + [vmem] * (len(outs) - 2),
-        scratch_shapes=[pltpu.VMEM(a.shape, a.dtype) for a in (*kept, pooled, image_grad)]
-        + [pltpu.SemaphoreType.DMA((2, PIECES, 2)), pltpu.SemaphoreType.DMA((len(kept),))],
-        compiler_params=pltpu.CompilerParams(vmem_limit_bytes=58 << 20),
+        scratch_shapes=[pltpu.SemaphoreType.DMA((2,))],
+        compiler_params=pltpu.CompilerParams(vmem_limit_bytes=16 << 20),
         name="final",
-    )(pooled, image_grad, *kept)
+    )(*(pltpu.with_memory_space_constraint(a, pltpu.VMEM) for a in (pooled, image_grad, *kept)))
     return (*results[0:2], *(a.T for a in results[2:12]), results[12])
 
 
@@ -968,12 +964,18 @@
         mask=hint_mask,
     )
     if fused:
-        small = (student_master, regress_master, mom_student, sq_student, mom_regress, sq_regress)
-        small = [a.T for a in small]
-        names = ("student_t", "regress_t", "mom_student", "sq_student", "mom_regress", "sq_regress")
-        arrays.update(zip(names, small))
-        parts = layer_pass(n, group, fused, dict(arrays, teacher_t=teacher_weight.T))
-        results = final_pass(*parts, *small, ema_student.T, ema_regress.T)
+        small = dict(
+            student_t=student_master,
+            regress_t=regress_master,
+            mom_student=mom_student,
+            sq_student=sq_student,
+            mom_regress=mom_regress,
+            sq_regress=sq_regress,
+            ema_student=ema_student,
+            ema_regress=ema_regress,
+        )
+        arrays.update({name: a.T for name, a in small.items()}, teacher_t=teacher_weight.T)
+        results = final_pass(*layer_pass(n, group, fused, arrays, tuple(small)))
         return (pool_win_like(results[0]), image_like(results[1]), *results[2:])
     arrays.update(gathered_filters(student_master, regress_master, teacher_weight))
     pooled, image_grad, student_part, regress_part = layer_pass(n, group, fused, arrays)

time: 143 us -> 139 us (0.972)
  Pallas kernels: 142 us -> 138 us
    pallas_call x1, Pallas kernels: 138 us -> 136 us  [layer_pass(): pl.pallas_call(functools.partial(layer_kernel, size, names), out_shape=li...]
where the time goes in v6:
time: 139 us
  Pallas kernels  138 us (99%)
    pallas_call x1, Pallas kernels, layer_pass(): pl.pallas_call(functools.partial(layer_kernel, size, names), out_shape=li...  136 us

profile of v6, /device:TPU:0, one launch (start us, length us, event | category | flops | bytes accessed | tf_op | source)
XLA Modules:
  0.0 139.0 jit_solution(700595962309616941)
XLA Ops:
  0.7 136.3 %layer.1 = (bf16[512,256]{1,0:T(8,128)(2,1)S(1)}, bf16[512,1024]{1,0:T(8,128)(2,1)S(1)}, f32[128,144]{1,0:T(8,128)S(1)}, f32[8,128]{1,0:T(8,128)S(1)}, f32[64,14...) custom-call(bf16[512,1024]{1,0:T(8,128)(2,1)} %bitcast.28, ...), custom_call_target="tpu_custom_call" | custom-call | flops 16307453952 | bytes 16777216 | tf_op jit(solution)/shard_map/layer/pallas_call | solution.py:831
  137.0 1.9 %final.1 = (bf16[512,256]{1,0:T(8,128)(2,1)}, bf16[512,1024]{1,0:T(8,128)(2,1)}, f32[64,144]{1,0:T(8,128)}, f32[64,144]{1,0:T(8,128)}, f32[64,144]{1,0:T(8,128)}...) custom-call(bf16[512,256]{1,0:T(8,128)(2,1)S(1)} %get-tuple-element., ...), custom_call_target="tpu_custom_call" | custom-call | tf_op jit(solution)/shard_map/final/pallas_call | solution.py:887

commit v7 on v6

--- a/solution.py
+++ b/solution.py
@@ -25,12 +25,8 @@
 CHUNK = IMG * IMG // STAGES
 LANES = 128
 AHEAD = 5
-NEAR_LATE = 3
-OUT_AT = 1
 ORDER = (2, 1, 3)
 EARLY = 2
-LOADS = 1
-CHIP_AT = 1
 
 
 def dot(left, right):
@@ -113,10 +109,7 @@
             for copy in loads[name]:
                 copy.start()
 
-    if LOADS == 0:
-        start_load(*sources)
-    else:
-        start_load("images", "swin")
+    start_load("images", "swin")
 
     for copy in small_loads:
         copy.start()
@@ -235,8 +228,8 @@
             ),
         )
 
-    def start_out(slot, steps=partners):
-        for step in steps:
+    def start_out(slot):
+        for step in partners:
             for copy in out_copies(slot, step):
                 copy.start()
 
@@ -289,8 +282,7 @@
     for j in range(r.wide.shape[0]):
         r.wide[j] = r.raw[:, j * LANES : (j + 1) * LANES].astype(F32)
     wait_load("swin")
-    if LOADS == 1:
-        start_load("twin", "pwin", "cot")
+    start_load("twin", "pwin", "cot")
     prepare(0, 0)
     pl.semaphore_wait(barrier, len(greeted))
     start_in(0, 0)
@@ -574,29 +566,18 @@
         stages(chunks(guess))
         wait_in(slot, 1)
         start_later(slot, 1)
-        if OUT_AT == 0 or not fused:
-            pl.when(last)(lambda: start_outs("early"))
+        pl.when(last)(lambda: start_outs("early"))
         stages(chunks(hints))
         stages(add_grads(r.rgrad, r.o_cols, r.hint), columns_of(r.hint, r.h_cols))
         if fused:
             pl.when(last)(lambda: start_core(0))
-            if OUT_AT == 1:
-                pl.when(last)(lambda: start_outs("early"))
         stages(chunks(pooling))
         stages(chunks(back))
-        if fused and CHIP_AT == 1:
+        if fused:
             pl.when(last)(lambda: step_chip(0))
         stages(add_grads(r.sgrad, r.x_cols, r.pre_grad), columns_of(r.pre_grad, r.p_cols))
         if fused:
-
-            def reduce_more():
-                start_core(1)
-                if OUT_AT == 2:
-                    start_outs("early")
-                if CHIP_AT == 0:
-                    step_chip(0)
-
-            pl.when(last)(reduce_more)
+            pl.when(last)(lambda: start_core(1))
         stages(chunks(image_back))
         if not fused:
 
@@ -628,8 +609,6 @@
             r.zs_send[step] = dot_nt(low_grad, r.spread[beside(step)]).astype(BF16)
             chan_copy(step).start()
         start_outs("mid")
-        far = [step for step in partners if step > NEAR_LATE]
-        start_out(slots - 1, far)
         total = dot_nt(
             r.whole_grad[...], r.spread[me].astype(F32), precision=lax.Precision.HIGHEST
         )
@@ -655,7 +634,7 @@
         r.part_chans[me] = tile
         for step in partners:
             chan_norm(step).start()
-        start_out(slots - 1, [step for step in partners if step not in far])
+        start_outs("late")
         for slot in out_order["mid"]:
             land(slot)
         for step in partners:
@@ -952,7 +931,7 @@
     ema_regress,
 ):
     image_like = lambda a: a.reshape(images.shape)
-    pool_win_like = lambda a: a.reshape(pool_win.shape)
+    pool_like = lambda a: a.reshape(pool_win.shape)
     depth = student_master.shape[0]
     fused = group % 2 == 0 and depth % 16 == 0
     arrays = dict(
@@ -976,7 +955,7 @@
         )
         arrays.update({name: a.T for name, a in small.items()}, teacher_t=teacher_weight.T)
         results = final_pass(*layer_pass(n, group, fused, arrays, tuple(small)))
-        return (pool_win_like(results[0]), image_like(results[1]), *results[2:])
+        return (pool_like(results[0]), image_like(results[1]), *results[2:])
     arrays.update(gathered_filters(student_master, regress_master, teacher_weight))
     pooled, image_grad, student_part, regress_part = layer_pass(n, group, fused, arrays)
     student_grad, regress_grad = scattered_grads(student_part, regress_part)
@@ -992,7 +971,7 @@
     ema_s = EMA_KEEP * ema_student + (1.0 - EMA_KEEP) * new_student
     ema_r = EMA_KEEP * ema_regress + (1.0 - EMA_KEEP) * new_regress
     return (
-        pool_win_like(pooled),
+        pool_like(pooled),
         image_like(image_grad),
         new_student,
         mom_s,

time: 139 us -> 138 us (level)
  no operation moved by 1% of the time
where the time goes in v7:
time: 138 us
  Pallas kernels  137 us (99%)
    pallas_call x1, Pallas kernels, layer_pass(): pl.pallas_call(functools.partial(layer_kernel, size, names), out_shape=li...  135 us

profile of v7, /device:TPU:0, one launch (start us, length us, event | category | flops | bytes accessed | tf_op | source)
XLA Modules:
  0.0 138.0 jit_solution(10856266306182338663)
XLA Ops:
  0.7 135.4 %layer.1 = (bf16[512,256]{1,0:T(8,128)(2,1)S(1)}, bf16[512,1024]{1,0:T(8,128)(2,1)S(1)}, f32[128,144]{1,0:T(8,128)S(1)}, f32[8,128]{1,0:T(8,128)S(1)}, f32[64,14...) custom-call(bf16[512,1024]{1,0:T(8,128)(2,1)} %bitcast.28, ...), custom_call_target="tpu_custom_call" | custom-call | flops 16307453952 | bytes 16777216 | tf_op jit(solution)/shard_map/layer/pallas_call | solution.py:810
  136.0 1.9 %final.1 = (bf16[512,256]{1,0:T(8,128)(2,1)}, bf16[512,1024]{1,0:T(8,128)(2,1)}, f32[64,144]{1,0:T(8,128)}, f32[64,144]{1,0:T(8,128)}, f32[64,144]{1,0:T(8,128)}...) custom-call(bf16[512,256]{1,0:T(8,128)(2,1)S(1)} %get-tuple-element., ...), custom_call_target="tpu_custom_call" | custom-call | tf_op jit(solution)/shard_map/final/pallas_call | solution.py:866
